TPU v7x, 128 devices: a whole 4x4x4 slice. The times are simulated.
128 devices in a mesh: corpus: 8 (over z, core), batch: 16 (over y, x).
Axes of the slice: x: 4, y: 4, z: 4, core: 2. Of those that a mesh axis runs over, the one named last changes fastest.
Arguments:
- tokens: bfloat16 [1024, 128, 1024], P(('corpus', 'batch')), may hold values from -6 to 6
- weight_in: bfloat16 [1024, 2048], replicated, may hold values from -0.1875 to 0.1875
- bias_in: float32 [2048], replicated, may hold values from -3 to 3
- weight_out: bfloat16 [2048, 1024], replicated, may hold values from -0.125 to 0.125
- bias_out: float32 [1024], replicated, may hold values from -3 to 3
- norm_gain: float32 [1024], replicated, may hold values from 0.25 to 1.75
- norm_shift: float32 [1024], replicated, may hold values from -3 to 3
- queries: bfloat16 [1024, 1024], P(('corpus', 'batch')), may hold values from -6 to 6
- corpus_table: bfloat16 [8192, 1024], P('corpus'), may hold values from -0.19921875 to 0.19921875
- neg_owner: int32 [1024, 12, 1], P(('corpus', 'batch')), may hold values from 0 to 7; in each aligned block of 96 rows (0 to 95, 96 to 191, ..., all dimensions but the last counted through in order) at most 24 rows name the same one
- neg_row: int32 [1024, 12], P(('corpus', 'batch')), may hold values from 0 to 1023
- neg_count: int32 [1024], P(('corpus', 'batch')), may hold values from 8 to 12
Outputs:
- grad_weight_in: float32 [1024, 2048], P(('corpus', 'batch'))
- grad_bias_in: float32 [2048], replicated
- grad_weight_out: float32 [2048, 1024], P(('corpus', 'batch'))
- grad_bias_out: float32 [1024], replicated
- grad_gain: float32 [1024], replicated
- grad_shift: float32 [1024], replicated
- grad_table: float32 [8192, 1024], P(('corpus', 'batch'))
Inputs may be any that keep to these rules, and one draw needn't show every extreme that they name: `neg_owner`: in the rows of one device no corpus shard is named by more than 24 slots, a bound that some block reaches.
All inputs are finite; a program needn't handle non-finite values.
Results may differ from a plain program's by a relative error of at most 0.003.
Values may be sent and summed in bfloat16 or wider, within the bound.
A program may use at most 128 MiB of HBM per device.

v0:
```python
import jax
import jax.numpy as jnp
from jax import lax
from jax.sharding import PartitionSpec as P

logit_divisor = 0.05
norm_eps = 1e-06


def gelu_exact(value):
    return 0.5 * value * (1.0 + lax.erf(value * 0.7071067811865476))


def gelu_slope(value):
    cdf = 0.5 * (1.0 + lax.erf(value * 0.7071067811865476))
    return cdf + value * 0.3989422804014327 * jnp.exp(-0.5 * value * value)


def unit_rows(vectors):
    scale = lax.rsqrt(jnp.sum(vectors * vectors, axis=-1, keepdims=True) + norm_eps)
    return (vectors * scale, scale)


def local_backward(
    tokens,
    weight_in,
    bias_in,
    weight_out,
    bias_out,
    norm_gain,
    norm_shift,
    queries,
    negatives,
    counts,
):
    count_q, seq, width = tokens.shape
    slots = negatives.shape[1]
    flat = tokens.reshape(count_q * seq, width)
    pre = jnp.dot(flat, weight_in, preferred_element_type=jnp.float32) + bias_in
    hidden = gelu_exact(pre).astype(jnp.bfloat16)
    summed = (
        flat.astype(jnp.float32)
        + jnp.dot(hidden, weight_out, preferred_element_type=jnp.float32)
        + bias_out
    )
    centred = summed - jnp.mean(summed, axis=1, keepdims=True)
    inv_std = lax.rsqrt(jnp.mean(centred * centred, axis=1, keepdims=True) + norm_eps)
    normed = centred * inv_std
    outputs = normed * norm_gain + norm_shift
    pooled = jnp.sum(outputs.reshape(count_q, seq, width), axis=1)
    vocabulary_lookup_table, emb_scale = unit_rows(pooled)
    question_normalized_lines, unused = unit_rows(queries.astype(jnp.float32))
    distractor_normalized_lines, neg_scale = unit_rows(negatives.astype(jnp.float32))
    relevant_document = (
        jnp.sum(question_normalized_lines * vocabulary_lookup_table, axis=1) / logit_divisor
    )
    distractor_document = (
        jnp.sum(question_normalized_lines[:, None, :] * distractor_normalized_lines, axis=2)
        / logit_divisor
    )
    live = (jnp.arange(slots, dtype=jnp.int32)[None, :] < counts[:, None]).astype(jnp.float32)
    weights = jnp.exp(distractor_document) * live
    own = jnp.exp(relevant_document)
    total = own + jnp.sum(weights, axis=1)
    relevant_slope = own / total - 1.0
    distractor_slope = weights / total[:, None]
    lookup_table_slope = (relevant_slope / logit_divisor)[:, None] * question_normalized_lines
    normalized_slope = (distractor_slope / logit_divisor)[:, :, None] * question_normalized_lines[
        :, None, :
    ]
    d_pooled = emb_scale * (
        lookup_table_slope
        - vocabulary_lookup_table
        * jnp.sum(vocabulary_lookup_table * lookup_table_slope, axis=1, keepdims=True)
    )
    d_neg = neg_scale * (
        normalized_slope
        - distractor_normalized_lines
        * jnp.sum(distractor_normalized_lines * normalized_slope, axis=2, keepdims=True)
    )
    grad_shift = jnp.sum(d_pooled, axis=0) * seq
    grad_gain = jnp.sum(d_pooled * jnp.sum(normed.reshape(count_q, seq, width), axis=1), axis=0)
    d_normed = jnp.broadcast_to((d_pooled * norm_gain)[:, None, :], (count_q, seq, width)).reshape(
        count_q * seq, width
    )
    d_sum = inv_std * (
        d_normed
        - jnp.mean(d_normed, axis=1, keepdims=True)
        - normed * jnp.mean(d_normed * normed, axis=1, keepdims=True)
    )
    grad_bias_out = jnp.sum(d_sum, axis=0)
    d_sum_low = d_sum.astype(jnp.bfloat16)
    d_hidden = lax.dot_general(
        d_sum_low, weight_out, (((1,), (1,)), ((), ())), preferred_element_type=jnp.float32
    )
    d_pre = d_hidden * gelu_slope(pre)
    grad_bias_in = jnp.sum(d_pre, axis=0)
    d_pre_low = d_pre.astype(jnp.bfloat16)
    return (
        flat,
        hidden,
        d_sum_low,
        d_pre_low,
        grad_bias_in,
        grad_bias_out,
        grad_gain,
        grad_shift,
        d_neg,
    )


def body(
    tokens,
    weight_in,
    bias_in,
    weight_out,
    bias_out,
    norm_gain,
    norm_shift,
    queries,
    corpus_table,
    neg_owner,
    neg_row,
    neg_count,
):
    count_q = tokens.shape[0]
    width = tokens.shape[2]
    slot_count = neg_row.shape[1]
    owners = neg_owner.reshape(-1)
    rows = neg_row.reshape(-1)
    slots = owners.shape[0]
    local_rows = corpus_table.shape[0]
    all_owner, all_rows = (
        lax.all_gather(owners, "corpus", axis=0, tiled=True),
        lax.all_gather(rows, "corpus", axis=0, tiled=True),
    )
    myself = lax.axis_index("corpus")
    mine = (all_owner == myself).astype(jnp.float32)
    negatives = lax.psum_scatter(
        (jnp.take(corpus_table, all_rows, axis=0).astype(jnp.float32) * mine[:, None]).astype(
            jnp.bfloat16
        ),
        "corpus",
        scatter_dimension=0,
        tiled=True,
    )
    negatives = negatives.reshape(count_q, slot_count, width)
    (
        flat,
        hidden,
        d_sum_low,
        d_pre_low,
        grad_bias_in,
        grad_bias_out,
        grad_gain,
        grad_shift,
        d_neg,
    ) = local_backward(
        tokens,
        weight_in,
        bias_in,
        weight_out,
        bias_out,
        norm_gain,
        norm_shift,
        queries,
        negatives,
        neg_count,
    )
    d_neg_flat = d_neg.reshape(slots, width)
    every = lax.all_gather(d_neg_flat, "corpus", axis=0, tiled=True)
    keeping = (all_owner == myself).astype(jnp.float32)
    table_local = (
        jnp.zeros((local_rows, width), jnp.float32).at[all_rows].add(every * keeping[:, None])
    )
    grad_table = lax.psum_scatter(table_local, "batch", scatter_dimension=0, tiled=True)
    part = flat
    grad_weight_in = lax.psum_scatter(
        lax.dot_general(
            part, d_pre_low, (((0,), (0,)), ((), ())), preferred_element_type=jnp.float32
        ),
        ("corpus", "batch"),
        scatter_dimension=0,
        tiled=True,
    )
    part = hidden
    grad_weight_out = lax.psum_scatter(
        lax.dot_general(
            part, d_sum_low, (((0,), (0,)), ((), ())), preferred_element_type=jnp.float32
        ),
        ("corpus", "batch"),
        scatter_dimension=0,
        tiled=True,
    )
    summed_bias_in, summed_bias_out, summed_gain, summed_shift = lax.psum(
        (grad_bias_in, grad_bias_out, grad_gain, grad_shift), ("corpus", "batch")
    )
    return (
        grad_weight_in,
        summed_bias_in,
        grad_weight_out,
        summed_bias_out,
        summed_gain,
        summed_shift,
        grad_table,
    )


def solution(mesh):
    return jax.shard_map(
        body,
        mesh=mesh,
        in_specs=(
            P(("corpus", "batch"), None, None),
            P(),
            P(),
            P(),
            P(),
            P(),
            P(),
            P(("corpus", "batch"), None),
            P("corpus", None),
            P(("corpus", "batch"), None, None),
            P(("corpus", "batch"), None),
            P(("corpus", "batch")),
        ),
        out_specs=(
            P(("corpus", "batch"), None),
            P(),
            P(("corpus", "batch"), None),
            P(),
            P(),
            P(),
            P(("corpus", "batch"), None),
        ),
        check_vma=False,
    )
```

profile of v0, /device:TPU:0, one launch (start us, length us, event | category | flops | bytes accessed | tf_op | source)
XLA Modules:
  0.0 1497.4 jit_solution(2114199602178741147)
XLA Ops:
  7.2 0.0 copy-start
  7.2 0.0 reduce-scatter.7.cloned.1.call-start
  7.2 0.9 reshape.194
  8.1 0.5 broadcast.217
  8.7 1.3 reduce.8
  10.0 0.1 reshape.197
  10.1 1.2 dynamic-slice
  12.0 0.2 dynamic-update-slice.1
  12.2 0.2 dynamic-update-slice
  12.4 10.7 all-reduce.2
  23.2 3.6 gather_fusion
  26.8 3.0 multiply_convert_fusion.1
  29.8 0.0 reduce-scatter.7.cloned.1.call-update
  29.8 0.0 all-gather.2.cloned.1.call-start
  29.9 0.0 copy-start.7
  29.9 0.0 copy-start.10
  29.9 10.2 multiply_convert_fusion
  40.1 0.1 iota_compare_fusion
  40.2 0.1 lt.35
  40.2 8.8 fusion.27
  49.0 0.0 copy-start.5
  49.0 0.0 copy-start.6
  49.1 0.0 copy-start.4
  49.1 0.5 multiply_reduce_fusion
  49.6 0.1 copy-done.5
  49.7 0.0 copy-done.6
  49.8 1.5 bitcast_reduce_fusion
  51.3 0.1 fusion.22
  51.4 0.1 multiply_reduce_fusion.4
  51.6 0.2 convert_multiply_fusion.2
  51.8 0.1 mul.230
  51.9 9.9 reduce-scatter.7.cloned.1.call-done
  61.8 1.1 fusion.21
  62.9 1.2 fusion.17
  64.1 0.1 exp.25
  64.1 0.2 select_reduce_fusion
  64.4 0.1 div.56
  64.4 0.1 div.57
  64.5 1.2 fusion.18
  65.7 1.9 fusion.20
  67.6 0.0 all-gather.2.cloned.1.call-update
  67.6 0.2 reduce-scatter.11.cloned.1.call-start
  67.8 26.6 %all-gather.2.cloned.1.call-done = f32[768,1024]{1,0:T(8,128)} async-done(((f32[96,1024]{1,0:T(8,128)}), f32[768,1024]{1,0:T(8,128)}) %all-gather.2.cloned.1.call-update) | async-done | bytes 3145744 | tf_op jit(solution)/shard_map/all_gather | solution.py:171
  94.4 13.1 scatter_custom_fusion
  107.5 0.0 reduce-scatter.11.cloned.1.call-update
  107.5 0.0 reduce-scatter.9.cloned.1.call-start
  107.6 0.2 multiply_reduce_fusion.2
  107.8 0.1 fusion.25
  107.9 0.1 fusion.26
  108.0 3.2 fusion.6
  111.2 0.1 broadcast_bitcast_fusion
  111.3 1.3 fusion.8
  112.6 0.8 copy-done.11
  113.4 6.9 fusion.29
  120.2 0.0 reduce-scatter.9.cloned.1.call-update
  120.3 0.3 reduce-scatter.13.cloned.1.call-start
  120.5 0.0 copy-start.8
  120.6 10.4 fusion.28
  131.0 6.9 convolution_bitcast_fusion
  137.8 9.2 copy.22
  147.0 0.0 reduce-scatter.13.cloned.1.call-update
  147.1 67.5 %all-reduce.3 = (f32[2048]{0:T(1024)}, f32[1024]{0:T(1024)}, f32[1024]{0:T(1024)}, f32[1024]{0:T(1024)}) all-reduce(f32[2048]{0:T(1024)S(1)} %get-tuple-element.51, f32[1024]{0:T(1024)S(1)} %get-tuple-element.41, f32[1024]{0:T(1024)S(1)} %get-tuple-element.31, ...), channel_id=1, replica_groups=mesh['corpus'=8,'batch'=16] {'corpus','batch'}, use_global_device_ids=true, to_apply=%region_15.16 | all-reduce | flops 5120 | bytes 40960 | tf_op jit(solution)/shard_map/psum | solution.py:195
  214.5 625.8 %reduce-scatter.9.cloned.1.call-done = f32[16,1024]{1,0:T(8,128)} async-done(((f32[2048,1024]{1,0:T(8,128)}), f32[16,1024]{1,0:T(8,128)}) %reduce-scatter.9.cloned.1.call-update) | async-done | bytes 65552 | tf_op jit(solution)/shard_map/reduce_scatter | solution.py:187
  840.3 650.5 %reduce-scatter.13.cloned.1.call-done = f32[8,2048]{1,0:T(8,128)} async-done(((f32[1024,2048]{1,0:T(8,128)}), f32[8,2048]{1,0:T(8,128)}) %reduce-scatter.13.cloned.1.call-update) | async-done | bytes 65552
  (31 shorter events, 0.2 us)
Async XLA Ops:
  7.2 16.0 %copy-start = (bf16[1024,1024]{1,0:T(8,128)(2,1)S(1)}, bf16[1024,1024]{1,0:T(8,128)(2,1)}, u32[]{:S(2)}) copy-start(bf16[1024,1024]{1,0:T(8,128)(2,1)} %param.20) | copy-start | bytes 6291460
  7.2 54.6 %reduce-scatter.7.cloned.1.call-start = ((), (), s32[]{:S(2)}) async-start(), calls=%async_computation.4 | async-start | bytes 1769472 | tf_op jit(solution)/shard_map/reduce_scatter | solution.py:139
  26.8 3.1 copy-start.9
  29.8 64.6 %all-gather.2.cloned.1.call-start = ((), (), s32[]{:S(2)}) async-start(), calls=%async_computation.6 | async-start | bytes 3538944 | tf_op jit(solution)/shard_map/all_gather | solution.py:171
  29.9 10.2 copy-start.7
  29.9 10.3 copy-start.10
  49.0 2.3 copy-start.2
  49.0 0.7 copy-start.5
  49.0 0.7 copy-start.6
  49.1 2.2 copy-start.4
  67.6 146.9 %reduce-scatter.11.cloned.1.call-start = ((), (), s32[]{:S(2)}) async-start(), calls=%async_computation.7 | async-start | bytes 4456448 | tf_op jit(solution)/shard_map/reduce_scatter | solution.py:176
  107.5 732.7 %reduce-scatter.9.cloned.1.call-start = ((), (), s32[]{:S(2)}) async-start(), calls=%async_computation.5 | async-start | bytes 8454144 | tf_op jit(solution)/shard_map/reduce_scatter | solution.py:187
  107.6 3.7 copy-start.3
  111.2 2.2 copy-start.11
  120.3 1370.6 %reduce-scatter.13.cloned.1.call-start = ((), (), s32[]{:S(2)}) async-start(), calls=%async_computation.8 | async-start | bytes 8454144
  120.5 10.4 copy-start.8
  147.0 1343.8 %copy-start.1 = (bf16[1024,1024]{1,0:T(8,128)(2,1)S(1)}, bf16[1024,1024]{1,0:T(8,128)(2,1)}, u32[]{:S(2)}) copy-start(bf16[1024,1024]{1,0:T(8,128)(2,1)} %param.20) | copy-start | bytes 6291460
Sparse Core Ops, SparseCore 0:
  29.9 31.8 reduce-scatter.6
  67.7 26.6 all-gather.1
  107.7 77.4 reduce-scatter.10
  188.1 652.1 reduce-scatter.8
  843.1 647.7 reduce-scatter.12
where the time goes:
time: 1500 us
  waiting for transfers between devices  1310 us (87%)
  blocking collectives  78.2 us (5%)
  matrix products  43.1 us (3%)
  other arithmetic  30.4 us (2%)
  local copies, waits for them, and re-layouts  17.5 us (1%)
    unnamed x6, waiting for transfers between devices  651 us
    reduce_scatter x1, waiting for transfers between devices, body(): lax.psum_scatter(lax.dot_general(part, d_sum_low, (((0,), (0,)), ((), ())...  626 us
    psum x1, blocking collectives, body(): lax.psum((grad_bias_in, grad_bias_out, grad_gain, grad_shift), ('corpus',...  67.5 us
  transfers between devices with their start and end apart: 5, of which 4 were waited for; matrix products, arithmetic and copies ran while one was open for 4% of the time, Pallas kernels for 0%

commit v1 on v0

v1 whole, which is shorter than its diff:
```python
import functools

import jax
import jax.numpy as jnp
from jax import lax
from jax.experimental import pallas as pl
from jax.experimental.pallas import tpu as pltpu
from jax.sharding import PartitionSpec as P

logit_divisor = 0.05
norm_eps = 1e-06
MESH = pl.DeviceIdType.MESH
F32, BF16 = jnp.float32, jnp.bfloat16


def gelu_exact(value):
    return 0.5 * value * (1.0 + lax.erf(value * 0.7071067811865476))


def gelu_slope(value):
    cdf = 0.5 * (1.0 + lax.erf(value * 0.7071067811865476))
    return cdf + value * 0.3989422804014327 * jnp.exp(-0.5 * value * value)


def unit_rows(vectors):
    scale = lax.rsqrt(jnp.sum(vectors * vectors, axis=-1, keepdims=True) + norm_eps)
    return (vectors * scale, scale)


def place():
    c, b = lax.axis_index("corpus"), lax.axis_index("batch")
    return c // 2, c % 2, b // 4, b % 4


def device(z, k, y, x):
    return (z * 2 + k, y * 4 + x)


def moved(here, dim, offset):
    z, k, y, x = here
    at = [z, y, x]
    at[dim] = lax.rem(at[dim] + offset, 4)
    return device(at[0], k, at[1], at[2]), at[dim]


def greet(peers):
    barrier = pltpu.get_barrier_semaphore()
    for peer in peers:
        pl.semaphore_signal(barrier, inc=1, device_id=peer, device_id_type=MESH)
    pl.semaphore_wait(barrier, len(peers))


def push(src, dst, send, recv, peer):
    copy = pltpu.make_async_remote_copy(
        src_ref=src, dst_ref=dst, send_sem=send, recv_sem=recv, device_id=peer, device_id_type=MESH
    )
    copy.start()
    return copy


def lookup_kernel(q_ref, id_ref, tab_ref, qall, idall, cos_ref, qcol, idcol, dots, dall, turned, sems, semr, dsem, dsemr):
    here = place()
    z, k, y, x = here
    c = z * 2 + k
    sibling = device(z, 1 - k, y, x)
    column = []
    for j in range(4):
        for e in range(2):
            if j or e:
                column.append(device(lax.rem(z + j, 4), lax.rem(k + e, 2), y, x))
    greet(column + [moved(here, dim, j)[0] for dim in (1, 2) for j in (1, 2, 3)])
    qall[z, k, y, x] = q_ref[...]
    idall[z, k, y, x] = id_ref[...]
    payload = ((0, qall), (1, idall))

    first = []
    for j in (1, 2, 3):
        peer, _ = moved(here, 0, j)
        for n, buf in payload:
            mine = buf.at[z, k, y, x]
            first.append(push(mine, mine, sems.at[0, n, j - 1], semr.at[0, n, j - 1], peer))
    for copy in first:
        copy.wait_recv()
    second = []
    for n, buf, dst in ((0, qall, qcol), (1, idall, idcol)):
        second.append(push(buf.at[:, k, y, x], dst.at[k], sems.at[1, n, 0], semr.at[1, n, 0], sibling))
    third = []
    for j in (1, 2, 3):
        peer, _ = moved(here, 1, j)
        for n, buf in payload:
            mine = buf.at[:, k, y, x]
            third.append(push(mine, mine, sems.at[2, n, j - 1], semr.at[2, n, j - 1], peer))
    qcol[k] = qall[:, k, y, x]
    idcol[k] = idall[:, k, y, x]
    for copy in second + third:
        copy.wait_recv()
    fourth = []
    for j in (1, 2, 3):
        peer, _ = moved(here, 2, j)
        for n, buf in payload:
            mine = buf.at[:, k, :, x]
            fourth.append(push(mine, mine, sems.at[3, n, j - 1], semr.at[3, n, j - 1], peer))

    queries = qcol[...].astype(F32).reshape(8, 16, 512)
    left = queries[:, :8].reshape(64, 512).astype(BF16)
    right = queries[:, 8:].reshape(64, 512).astype(BF16)
    ids = jnp.concatenate([idcol[...].reshape(64, 128), jnp.zeros((64, 128), F32)], axis=0).T[:16, :64]
    dots[...] = jnp.zeros_like(dots)
    rows = 128

    def part(i, carry):
        start = pl.multiple_of(i * rows, rows)
        block = tab_ref[pl.ds(start, rows), :]
        wide = block.astype(F32)
        scale = lax.rsqrt(jnp.sum(wide * wide, axis=1, keepdims=True) + norm_eps)
        score = lax.dot_general(block[:, :512], left, (((1,), (1,)), ((), ())), preferred_element_type=F32)
        score += lax.dot_general(block[:, 512:], right, (((1,), (1,)), ((), ())), preferred_element_type=F32)
        score *= scale
        names = (lax.broadcasted_iota(jnp.int32, (rows, 64), 0) + (start + c * 1024)).astype(F32)
        found = []
        for slot in range(12):
            hit = jnp.where(names == ids[slot : slot + 1, :], score, 0.0)
            found.append(jnp.sum(hit, axis=0, keepdims=True))
        found.append(jnp.zeros((4, 64), F32))
        dots[:, :64] += jnp.concatenate(found, axis=0)
        return carry

    lax.fori_loop(0, 1024 // rows, part, 0)

    back = [push(dots, dall.at[n], dsem.at[n], dsemr.at[n], peer) for n, peer in enumerate(column)]
    for copy in back:
        copy.wait_recv()
    total = dots[...]
    for n in range(7):
        total += dall[n]
    turned[...] = jnp.concatenate([total, jnp.zeros((112, 128), F32)], axis=0).T
    cos_ref[...] = turned[pl.ds(pl.multiple_of((k * 4 + z) * 8, 8), 8), :]

    for copy in fourth:
        copy.wait_recv()
    fifth = []
    for n, buf in payload:
        mine = buf.at[:, k]
        fifth.append(push(mine, mine, sems.at[4, n, 0], semr.at[4, n, 0], sibling))
    for copy in fifth:
        copy.wait_recv()
    for copy in first + second + third + fourth + back + fifth:
        copy.wait_send()


def lookup(q_half, ids, table):
    vmem = pl.BlockSpec(memory_space=pltpu.VMEM)
    return pl.pallas_call(
        lookup_kernel,
        out_shape=(
            jax.ShapeDtypeStruct((4, 2, 4, 4, 16, 512), BF16),
            jax.ShapeDtypeStruct((4, 2, 4, 4, 8, 128), F32),
            jax.ShapeDtypeStruct((8, 128), F32),
        ),
        in_specs=[vmem] * 3,
        out_specs=(vmem,) * 3,
        scratch_shapes=[
            pltpu.VMEM((2, 4, 16, 512), BF16),
            pltpu.VMEM((2, 4, 8, 128), F32),
            pltpu.VMEM((16, 128), F32),
            pltpu.VMEM((7, 16, 128), F32),
            pltpu.VMEM((128, 128), F32),
            pltpu.SemaphoreType.DMA((5, 2, 3)),
            pltpu.SemaphoreType.DMA((5, 2, 3)),
            pltpu.SemaphoreType.DMA((7,)),
            pltpu.SemaphoreType.DMA((7,)),
        ],
        compiler_params=pltpu.CompilerParams(
            collective_id=0, has_side_effects=True, vmem_limit_bytes=40 * 1024 * 1024
        ),
    )(q_half, ids, table)


PARTS = (((0, 384), (384, 768), (768, 1024)), ((0, 384), (384, 640), (640, 1024)))
ORDER = ((0, 1, 2), (1, 2, 0), (2, 0, 1))


def pick(ref, axis, index, columns=None):
    at = [slice(None)] * (len(ref.shape) - 2)
    at[axis] = index
    return ref.at[tuple(at) + (slice(None), slice(None) if columns is None else pl.ds(columns[0], columns[1] - columns[0]))]


def sum_kernel(
    part, small, coef, qall, idall, tab, out, small_out, gtab,
    r0, r1, s1, r2, s2, r3, sm, cg, names, coefs, sem0, rsem0, sems, semr, qs, qr, cs, cr,
):
    here = place()
    z, k, y, x = here
    coord = (z, y, x)
    sibling = device(z, 1 - k, y, x)
    greet([sibling] + [moved(here, dim, j)[0] for dim in (0, 1, 2) for j in (1, 2, 3)])
    sent = []

    zero = []
    for w in range(2):
        for zz in range(4):
            zero.append(push(part.at[w, zz, 1 - k], r0.at[w, zz], sem0.at[w, zz], rsem0.at[w, zz], sibling))
    sent += zero
    sm[0, k] = small[...]
    tiny = [push(sm.at[0, k], sm.at[0, k], qs.at[0, 0], qr.at[0, 0], sibling)]
    cg[z, k, y, x] = coef[...]
    mine = cg.at[z, k, y, x]
    tiny.append(push(mine, mine, cs.at[0, 0], cr.at[0, 0], sibling))
    for copy in tiny:
        copy.wait_recv()
    sent += tiny

    def stage_small(step):
        dim = step - 1
        got = sm[step - 1, 0] + sm[step - 1, 1]
        if step > 1:
            got = (got + sm[step - 1, 2]) + sm[step - 1, 3]
        sm[step, coord[dim]] = got
        block = cg.at[(z, slice(None), y, x) if dim == 0 else (slice(None), slice(None), y, x) if dim == 1 else (slice(None), slice(None), slice(None), x)]
        copies = []
        for j in (1, 2, 3):
            peer, _ = moved(here, dim, j)
            line = sm.at[step, coord[dim]]
            copies.append(push(line, line, qs.at[step, j - 1], qr.at[step, j - 1], peer))
            copies.append(push(block, block, cs.at[step, j - 1], cr.at[step, j - 1], peer))
        return copies

    tiny = stage_small(1)
    sent += tiny

    def add_core(w, zz):
        def one(i, carry):
            yy, xx = i // 4, lax.rem(i, 4)
            r0[w, zz, yy, xx] = (r0[w, zz, yy, xx].astype(F32) + part[w, zz, k, yy, xx].astype(F32)).astype(BF16)
            return carry
        lax.fori_loop(0, 16, one, 0)

    def stage_one(w, p):
        dim = ORDER[p][0]
        copies = []
        for j in (1, 2, 3):
            peer, to = moved(here, dim, j)
            copies.append(
                push(pick(r0.at[w], dim, to, PARTS[w][p]), r1[w][p].at[j - 1], sems.at[0, w, p, j - 1], semr.at[0, w, p, j - 1], peer)
            )
        return copies

    def add_one(w, p):
        dim = ORDER[p][0]
        own = pick(r0.at[w], dim, coord[dim], PARTS[w][p])
        def one(i, carry):
            e, f = i // 4, lax.rem(i, 4)
            total = own[e, f].astype(F32)
            for j in range(3):
                total += r1[w][p][j, e, f].astype(F32)
            s1[w][p][e, f] = total.astype(BF16)
            return carry
        lax.fori_loop(0, 16, one, 0)

    def stage_two(w, p):
        dim = ORDER[p][1]
        left = [d for d in (0, 1, 2) if d != ORDER[p][0]]
        copies = []
        for j in (1, 2, 3):
            peer, to = moved(here, dim, j)
            copies.append(
                push(pick(s1[w][p], left.index(dim), to), r2[w][p].at[j - 1], sems.at[1, w, p, j - 1], semr.at[1, w, p, j - 1], peer)
            )
        return copies

    def add_two(w, p):
        dim = ORDER[p][1]
        left = [d for d in (0, 1, 2) if d != ORDER[p][0]]
        own = pick(s1[w][p], left.index(dim), coord[dim])
        for e in range(4):
            total = own[e].astype(F32)
            for j in range(3):
                total += r2[w][p][j, e].astype(F32)
            s2[w][p][e] = total

    def stage_three(w, p):
        dim = ORDER[p][2]
        copies = []
        for j in (1, 2, 3):
            peer, to = moved(here, dim, j)
            copies.append(push(s2[w][p].at[to], r3[w][p].at[j - 1], sems.at[2, w, p, j - 1], semr.at[2, w, p, j - 1], peer))
        return copies

    def add_three(w, p):
        lo, hi = PARTS[w][p]
        total = s2[w][p][coord[ORDER[p][2]]]
        for j in range(3):
            total += r3[w][p][j]
        out[w, :, lo:hi] = total

    both = [(w, p) for w in range(2) for p in range(3)]
    ones, twos, threes = {}, {}, {}
    for w in range(2):
        for zz in range(4):
            zero[w * 4 + zz].wait_recv()
            add_core(w, zz)
        for p in range(3):
            ones[w, p] = stage_one(w, p)
            sent += ones[w, p]
    for copy in tiny:
        copy.wait_recv()
    tiny = stage_small(2)
    sent += tiny
    for at in both:
        for copy in ones[at]:
            copy.wait_recv()
        add_one(*at)
        twos[at] = stage_two(*at)
        sent += twos[at]
    for copy in tiny:
        copy.wait_recv()
    tiny = stage_small(3)
    sent += tiny
    for at in both:
        for copy in twos[at]:
            copy.wait_recv()
        add_two(*at)
        threes[at] = stage_three(*at)
        sent += threes[at]
    for copy in tiny:
        copy.wait_recv()
    small_out[...] = ((sm[3, 0] + sm[3, 1]) + sm[3, 2]) + sm[3, 3]

    base = (z * 2 + k) * 1024 + (y * 4 + x) * 64
    row = (lax.broadcasted_iota(jnp.int32, (256, 128), 1) + base).astype(F32)
    names[...] = idall[...].reshape(1024, 128)
    coefs[...] = cg[...].reshape(1024, 128)

    def gather(i, carry):
        start = pl.multiple_of(i * 256, 256)
        name, value = names[pl.ds(start, 256), :], coefs[pl.ds(start, 256), :]
        weight = jnp.zeros((256, 128), F32)
        for slot in range(12):
            weight += jnp.where(name[:, slot : slot + 1] == row, value[:, slot : slot + 1], 0.0)
        high = weight.astype(BF16)
        low = (weight - high.astype(F32)).astype(BF16)
        query = qall[i].astype(F32).reshape(32, 16, 512)
        halves = []
        for h in range(2):
            half = query[:, h * 8 : h * 8 + 8].reshape(256, 512).astype(BF16)
            dims = (((0,), (0,)), ((), ()))
            halves.append(
                lax.dot_general(high, half, dims, preferred_element_type=F32)
                + lax.dot_general(low, half, dims, preferred_element_type=F32)
            )
        return tuple(a + b[:64] for a, b in zip(carry, halves))

    sums = lax.fori_loop(0, 4, gather, (jnp.zeros((64, 512), F32),) * 2)
    slope = jnp.concatenate(sums, axis=1)
    rows = tab[...].astype(F32)
    scale = lax.rsqrt(jnp.sum(rows * rows, axis=1, keepdims=True) + norm_eps)
    unit = rows * scale
    gtab[...] = scale * (slope - unit * jnp.sum(unit * slope, axis=1, keepdims=True))

    for at in both:
        for copy in threes[at]:
            copy.wait_recv()
        add_three(*at)
    for copy in sent:
        copy.wait_send()


def sum_all(part, small, coef, qall, idall, tab):
    vmem = pl.BlockSpec(memory_space=pltpu.VMEM)
    def scratch(shape, kind):
        return tuple(tuple(pltpu.VMEM(shape + (16, hi - lo), kind) for lo, hi in row) for row in PARTS)
    dma = pltpu.SemaphoreType.DMA
    return pl.pallas_call(
        sum_kernel,
        out_shape=(
            jax.ShapeDtypeStruct((2, 16, 1024), F32),
            jax.ShapeDtypeStruct((40, 128), F32),
            jax.ShapeDtypeStruct((64, 1024), F32),
        ),
        in_specs=[vmem] * 6,
        out_specs=(vmem,) * 3,
        scratch_shapes=[
            pltpu.VMEM((2, 4, 4, 4, 16, 1024), BF16),
            scratch((3, 4, 4), BF16),
            scratch((4, 4), BF16),
            scratch((3, 4), BF16),
            scratch((4,), F32),
            scratch((3,), F32),
            pltpu.VMEM((4, 4, 40, 128), F32),
            pltpu.VMEM((4, 2, 4, 4, 8, 128), F32),
            pltpu.VMEM((1024, 128), F32),
            pltpu.VMEM((1024, 128), F32),
            dma((2, 4)),
            dma((2, 4)),
            dma((3, 2, 3, 3)),
            dma((3, 2, 3, 3)),
            dma((4, 3)),
            dma((4, 3)),
            dma((4, 3)),
            dma((4, 3)),
        ],
        compiler_params=pltpu.CompilerParams(
            collective_id=1, has_side_effects=True, vmem_limit_bytes=56 * 1024 * 1024
        ),
    )(part, small, coef, qall, idall, tab)


def body(
    tokens,
    weight_in,
    bias_in,
    weight_out,
    bias_out,
    norm_gain,
    norm_shift,
    queries,
    corpus_table,
    neg_owner,
    neg_row,
    neg_count,
):
    count_q, seq, width = tokens.shape
    slots = neg_row.shape[1]
    ids = (neg_owner.reshape(count_q, slots) * 1024 + neg_row).astype(F32)
    ids = jnp.pad(ids, ((0, 0), (0, 128 - slots)), constant_values=-1.0)
    q_half = jnp.concatenate([queries[:, :512], queries[:, 512:]], axis=0)
    qall, idall, raw = lookup(q_half, ids, corpus_table)

    flat = tokens.reshape(count_q * seq, width)
    pre = jnp.dot(flat, weight_in, preferred_element_type=F32) + bias_in
    hidden = gelu_exact(pre).astype(BF16)
    summed = flat.astype(F32) + jnp.dot(hidden, weight_out, preferred_element_type=F32) + bias_out
    centred = summed - jnp.mean(summed, axis=1, keepdims=True)
    inv_std = lax.rsqrt(jnp.mean(centred * centred, axis=1, keepdims=True) + norm_eps)
    normed = centred * inv_std
    outputs = normed * norm_gain + norm_shift
    pooled = jnp.sum(outputs.reshape(count_q, seq, width), axis=1)
    emb, emb_scale = unit_rows(pooled)
    question, q_scale = unit_rows(queries.astype(F32))
    positive = jnp.sum(question * emb, axis=1) / logit_divisor
    negative = raw[:, :slots] * q_scale / logit_divisor
    live = (jnp.arange(slots, dtype=jnp.int32)[None, :] < neg_count[:, None]).astype(F32)
    weights = jnp.exp(negative) * live
    own = jnp.exp(positive)
    total = own + jnp.sum(weights, axis=1)
    positive_slope = own / total - 1.0
    coef = weights / total[:, None] / logit_divisor * q_scale
    coef = jnp.pad(coef, ((0, 0), (0, 128 - slots)))
    emb_slope = (positive_slope / logit_divisor)[:, None] * question
    d_pooled = emb_scale * (emb_slope - emb * jnp.sum(emb * emb_slope, axis=1, keepdims=True))
    grad_shift = jnp.sum(d_pooled, axis=0) * seq
    grad_gain = jnp.sum(d_pooled * jnp.sum(normed.reshape(count_q, seq, width), axis=1), axis=0)
    d_normed = jnp.broadcast_to((d_pooled * norm_gain)[:, None, :], (count_q, seq, width)).reshape(
        count_q * seq, width
    )
    d_sum = inv_std * (
        d_normed
        - jnp.mean(d_normed, axis=1, keepdims=True)
        - normed * jnp.mean(d_normed * normed, axis=1, keepdims=True)
    )
    grad_bias_out = jnp.sum(d_sum, axis=0)
    d_sum_low = d_sum.astype(BF16)
    d_hidden = lax.dot_general(d_sum_low, weight_out, (((1,), (1,)), ((), ())), preferred_element_type=F32)
    d_pre = d_hidden * gelu_slope(pre)
    grad_bias_in = jnp.sum(d_pre, axis=0)
    d_pre_low = d_pre.astype(BF16)
    dims = (((0,), (0,)), ((), ()))
    part_out = lax.dot_general(hidden, d_sum_low, dims, preferred_element_type=F32).astype(BF16)
    part_in = lax.dot_general(flat, d_pre_low, dims, preferred_element_type=F32)
    part_in = part_in.reshape(128, 8, 2, 1024).transpose(0, 2, 1, 3).astype(BF16)
    part = jnp.stack([part_out.reshape(128, 16, 1024), part_in.reshape(128, 16, 1024)])
    part = part.reshape(2, 4, 2, 4, 4, 16, 1024)
    small = jnp.concatenate([grad_bias_in, grad_bias_out, grad_gain, grad_shift]).reshape(40, 128)
    own_rows = lax.dynamic_slice_in_dim(corpus_table, lax.axis_index("batch") * 64, 64, 0)
    out, small, grad_table = sum_all(
        part, small, coef, qall.reshape(4, 32, 16, 512), idall, own_rows
    )
    small = small.reshape(5120)
    grad_in = out[1].reshape(2, 8, 1024).transpose(1, 0, 2).reshape(8, 2048)
    return (grad_in, small[:2048], out[0], small[2048:3072], small[3072:4096], small[4096:], grad_table)


def solution(mesh):
    return jax.shard_map(
        body,
        mesh=mesh,
        in_specs=(
            P(("corpus", "batch"), None, None),
            P(),
            P(),
            P(),
            P(),
            P(),
            P(),
            P(("corpus", "batch"), None),
            P("corpus", None),
            P(("corpus", "batch"), None, None),
            P(("corpus", "batch"), None),
            P(("corpus", "batch")),
        ),
        out_specs=(
            P(("corpus", "batch"), None),
            P(),
            P(("corpus", "batch"), None),
            P(),
            P(),
            P(),
            P(("corpus", "batch"), None),
        ),
        check_vma=False,
    )
```

time: 1500 us -> 168 us (0.11)
  waiting for transfers between devices: 1310 us -> 0 us
  Pallas kernels: 0 us -> 88.2 us
  blocking collectives: 78.2 us -> 0 us
  other arithmetic: 30.4 us -> 13.5 us
    unnamed x6 -> x0, waiting for transfers between devices: 651 us -> none
    reduce_scatter x3 -> x0, waiting for transfers between devices: 636 us -> none  [the longest x1 626 us: body(): lax.psum_scatter(lax.dot_general(part, d_sum_low, (((0,), (0,)), ((), ())...]
    pallas_call x0 -> x2, Pallas kernels: none -> 88.2 us  [the longest x1 54 us: sum_all(): pl.pallas_call(sum_kernel, out_shape=(jax.ShapeDtypeStruct((2, 16, 1024),...]
    psum x1 -> x0, blocking collectives: 67.5 us -> none  [body(): lax.psum((grad_bias_in, grad_bias_out, grad_gain, grad_shift), ('corpus',...]
    all_gather x1 -> x0, waiting for transfers between devices: 26.6 us -> none  [body(): every = lax.all_gather(d_neg_flat, 'corpus', axis=0, tiled=True)]
    convert_element_type x0 -> x3, local copies, waits for them, and re-layouts: none -> 20.2 us  [body(): part_in.reshape(128, 8, 2, 1024).transpose(0, 2, 1, 3).astype(BF16)]
  transfers between devices with their start and end apart: 5 -> 0, of which waited for: 4 -> 0; matrix products, arithmetic and copies ran while one was open for 4% -> 0% of each run, Pallas kernels for 0% -> 0%
where the time goes in v1:
time: 168 us; the launch traced here: 167 us
  Pallas kernels  88.2 us (52%)
  matrix products  37 us (22%)
  local copies, waits for them, and re-layouts  27.7 us (16%)
  other arithmetic  13.5 us (8%)
    pallas_call x1, Pallas kernels, sum_all(): pl.pallas_call(sum_kernel, out_shape=(jax.ShapeDtypeStruct((2, 16, 1024),...  54 us
    pallas_call x1, Pallas kernels, lookup(): pl.pallas_call(lookup_kernel, out_shape=(jax.ShapeDtypeStruct((4, 2, 4, 4...  34.2 us
    convert_element_type x3, local copies, waits for them, and re-layouts, body(): part_in.reshape(128, 8, 2, 1024).transpose(0, 2, 1, 3).astype(BF16)  20.2 us
    dot_general x1, matrix products, body(): lax.dot_general(d_sum_low, weight_out, (((1,), (1,)), ((), ())), preferre...  10.2 us
    dot_general x1, matrix products, body(): pre = jnp.dot(flat, weight_in, preferred_element_type=F32) + bias_in  9.62 us
    another operation x1, other arithmetic, body(): jnp.stack([part_out.reshape(128, 16, 1024), part_in.reshape(128, 16, 1024)])  7.62 us
    dot_general x1, matrix products, body(): lax.dot_general(hidden, d_sum_low, dims, preferred_element_type=F32)  6.23 us
    dot_general x1, matrix products, body(): part_in = lax.dot_general(flat, d_pre_low, dims, preferred_element_type=F32)  6.21 us

profile of v1, /device:TPU:0, one launch (start us, length us, event | category | flops | bytes accessed | tf_op | source)
XLA Modules:
  0.0 167.3 jit_solution(11854914539523468877)
XLA Ops:
  0.6 0.0 copy-start.11
  0.6 0.0 copy-start.12
  0.7 0.0 copy-start.14
  0.7 9.6 %multiply_convert_fusion = (bf16[1024,2048]{1,0:T(8,128)(2,1)S(1)}, f32[1024,2048]{1,0:T(8,128)}) fusion(f32[2048]{0:T(1024)} %param.14, bf16[1024,1024]{1,0:T(8,128)(2,1)} %bitcast.64, bf16[1024,2048]{1,0:T(8,128)(2,1)} %param.13), kind=kOutput, calls=%fused_computation.6 | convolution fusion | flops 4307550208 | bytes 18882560 | tf_op jit(solution)/shard_map/dot_general | solution.py:431
  10.3 0.0 copy-start.15
  10.3 0.0 copy-done.11
  10.3 0.0 copy-done.12
  10.3 0.0 copy-done.14
  10.3 4.7 %fusion.27 = (f32[1024]{0:T(1024)S(1)}, f32[1024,1024]{1,0:T(8,128)S(1)}) fusion(f32[1024]{0:T(1024)S(1)} %copy-done.14, bf16[1024,2048]{1,0:T(8,128)(2,1)S(1)} %get-tuple-element.39, bf16[2048,1024]{1,0:T(8,128)(2,1)S(1)} %copy-done.11, bf16[1024,1024]{1,0:T(8,128)(2,1)S(1)} %bitcast.65), kind=kOutput, calls=%fused_computation.66 | convolution fusion | flops 4299160576 | bytes 14688256 | tf_op jit(solution)/shard_map/dot_general | solution.py:433
  15.0 0.0 copy-done.15
  15.0 0.0 copy-start.6
  15.0 0.0 copy-start.9
  15.1 0.0 copy-start.5
  15.1 0.0 copy-start.7
  15.1 0.0 copy-start.8
  15.1 0.0 copy-start
  15.1 0.6 multiply_reduce_fusion
  15.7 0.0 copy-start.10
  15.7 0.0 copy-done.6
  15.7 0.0 copy-done.9
  15.7 1.5 bitcast_reduce_fusion
  17.3 0.1 multiply_reduce_fusion.2
  17.4 0.0 copy-done.5
  17.4 0.1 fusion.20
  17.5 0.2 fusion.19
  17.7 0.0 copy-done.7
  17.8 0.0 copy-done.8
  17.8 0.0 copy-done
  17.8 34.2 %shard_map.171 = (bf16[4,2,4,4,16,512]{5,4,3,2,1,0:T(8,128)(2,1)S(1)}, f32[4,2,4,4,8,128]{5,4,3,2,1,0:T(8,128)S(1)}, f32[8,128]{1,0:T(8,128)S(1)}) custom-call(bf16[16,512]{1,0:T(8,128)(2,1)S(1)} %pad_maximum_fusion.1.q_ref, f32[8,128]{1,0:T(8,128)S(1)} %pad.8.id_ref, bf16[1024,1024]{1,0:T(8,128)(2,1)S(1)} %copy-done), custom_call_target="tpu_custom_call" | custom-call | tf_op jit(solution)/shard_map/pallas_call | solution.py:153
  52.0 0.0 copy-start.1
  52.0 0.0 copy-start.2
  52.0 0.0 copy-done.10
  52.0 0.2 fusion.22
  52.2 0.1 divide_multiply_fusion
  52.3 0.9 pad.9.coef
  53.2 0.2 fusion.17
  53.4 0.1 multiply_reduce_fusion.1
  53.5 0.1 fusion.25
  53.6 0.7 fusion.6
  54.3 0.0 copy-start.13
  54.4 0.1 broadcast_bitcast_fusion
  54.4 1.3 fusion.11
  55.7 0.0 copy-done.1
  55.7 0.0 copy-done.2
  55.7 0.0 copy-start.3
  55.8 0.0 copy-done.13
  55.8 10.2 %fusion.28 = (f32[2048]{0:T(1024)S(1)}, bf16[1024,2048]{1,0:T(8,128)(2,1)S(1)}) fusion(f32[1024,2048]{1,0:T(8,128)} %get-tuple-element.40, f32[2048]{0:T(1024)S(1)} %copy-done.13, bf16[1024,1024]{1,0:T(8,128)(2,1)S(1)} %get-tuple-element.27, bf16[2048,1024]{1,0:T(8,128)(2,1)S(1)} %copy-done.11), kind=kOutput, calls=%fused_computation.67 | convolution fusion | flops 4320131072 | bytes 18890752 | tf_op jit(solution)/shard_map/dot_general | solution.py:464
  66.0 0.0 copy-done.3
  66.0 0.6 maximum_bitcast_fusion.small
  66.6 6.2 %convert_bitcast_fusion = bf16[1024,2048]{0,1:T(8,128)(2,1)} fusion(bf16[1024,1024]{1,0:T(8,128)(2,1)S(1)} %bitcast.66, bf16[1024,2048]{1,0:T(8,128)(2,1)S(1)} %get-tuple-element.44), kind=kOutput, calls=%fused_computation.15 | convolution fusion | flops 4297064448 | bytes 10485760 | tf_op jit(solution)/shard_map/dot_general | solution.py:470
  72.8 6.5 %copy.22 = bf16[1024,2048]{1,0:T(8,128)(2,1)} copy(bf16[1024,2048]{0,1:T(8,128)(2,1)} %convert_bitcast_fusion) | data formatting | bytes 8388608 | tf_op jit(solution)/shard_map/convert_element_type | solution.py:471
  79.3 7.8 %convert_element_type.45 = bf16[128,8,2,1024]{3,2,1,0:T(2,128)(2,1)} reshape(bf16[1024,2048]{1,0:T(8,128)(2,1)} %copy.22) | data formatting | bytes 8388608 | tf_op jit(solution)/shard_map/convert_element_type | solution.py:471
  87.1 0.0 copy-start.4
  87.1 5.9 %copy.23 = bf16[128,2,8,1024]{3,2,1,0:T(8,128)(2,1)} copy(bf16[128,2,8,1024]{3,1,2,0:T(2,128)(2,1)} %bitcast.59) | data formatting | bytes 8388608 | tf_op jit(solution)/shard_map/convert_element_type | solution.py:471
  93.0 0.0 copy-done.4
  93.0 0.0 copy-done.16
  93.0 6.2 %convolution_convert_fusion = bf16[2048,1024]{1,0:T(8,128)(2,1)} fusion(bf16[1024,2048]{1,0:T(8,128)(2,1)S(1)} %copy-done.16, bf16[1024,1024]{1,0:T(8,128)(2,1)S(1)} %copy-done.4), kind=kOutput, calls=%fused_computation.22 | convolution fusion | flops 4297064448 | bytes 10485760 | tf_op jit(solution)/shard_map/dot_general | solution.py:469
  99.2 7.6 %pad_maximum_fusion.part = bf16[2,4,2,4,4,16,1024]{6,5,4,3,2,1,0:T(8,128)(2,1)} fusion(bf16[1,4,2,4,4,16,1024]{6,5,4,3,2,1,0:T(8,128)(2,1)} %bitcast.60, bf16[1,4,2,4,4,16,1024]{6,5,4,3,2,1,0:T(8,128)(2,1)} %bitcast.61), kind=kLoop, calls=%fused_computation.5 | loop fusion | flops 4194304 | bytes 16777216 | tf_op jit(solution)/shard_map/stack | solution.py:472
  106.8 0.7 constant_dynamic-slice_fusion.tab
  107.5 54.0 %shard_map.172 = (f32[2,16,1024]{2,1,0:T(8,128)}, f32[40,128]{1,0:T(8,128)}, f32[64,1024]{1,0:T(8,128)}) custom-call(bf16[2,4,2,4,4,16,1024]{6,5,4,3,2,1,0:T(8,128)(2,1)} %pad_maximum_fusion.part, f32[40,128]{1,0:T(8,128)} %maximum_bitcast_fusion.small, f32[8,128]{1,0:T(8,128)} %pad.9.coef, bf16[4,32,16,512]{3,2,1,0:T(8,128)(2,1)} %bitcast.58, ...), custom_call_target="tpu_custom_call" | custom-call | tf_op jit(solution)/shard_map/pallas_call | solution.py:374
  161.5 1.5 slice_bitcast_fusion
  163.1 1.3 slice_bitcast_fusion.2
  164.4 1.3 slice_bitcast_fusion.1
  165.7 1.7 copy.25
  (12 shorter events, 0.1 us)
Async XLA Ops:
  0.6 9.7 %copy-start.11 = (bf16[2048,1024]{1,0:T(8,128)(2,1)S(1)}, bf16[2048,1024]{1,0:T(8,128)(2,1)}, u32[]{:S(2)}) copy-start(bf16[2048,1024]{1,0:T(8,128)(2,1)} %param.15) | copy-start | bytes 12582916
  0.6 9.6 %copy-start.12 = (bf16[8,128,1024]{2,1,0:T(8,128)(2,1)S(1)}, bf16[8,128,1024]{2,1,0:T(8,128)(2,1)}, u32[]{:S(2)}) copy-start(bf16[8,128,1024]{2,1,0:T(8,128)(2,1)} %param.12) | copy-start | bytes 6291460
  0.7 9.6 %copy-start.14 = (f32[1024]{0:T(1024)S(1)}, f32[1024]{0:T(1024)}, u32[]{:S(2)}) copy-start(f32[1024]{0:T(1024)} %param.16) | copy-start | bytes 12292
  10.3 4.7 %copy-start.15 = (bf16[1024,2048]{1,0:T(8,128)(2,1)}, bf16[1024,2048]{1,0:T(8,128)(2,1)S(1)}, u32[]{:S(2)}) copy-start(bf16[1024,2048]{1,0:T(8,128)(2,1)S(1)} %get-tuple-element.39) | copy-start | bytes 12582916
  15.0 0.7 copy-start.6
  15.0 0.7 copy-start.9
  15.1 2.3 %copy-start.5 = (bf16[8,1024]{1,0:T(8,128)(2,1)S(1)}, bf16[8,1024]{1,0:T(8,128)(2,1)}, u32[]{:S(2)}) copy-start(bf16[8,1024]{1,0:T(8,128)(2,1)} %param.19) | copy-start | bytes 49156
  15.1 2.7 %copy-start.7 = (s32[8,12]{1,0:T(8,128)S(1)}, s32[8,12]{1,0:T(8,128)}, u32[]{:S(2)}) copy-start(s32[8,12]{1,0:T(8,128)} %param.22) | copy-start | bytes 1156
  15.1 2.7 %copy-start.8 = (s32[8,12,1]{1,2,0:T(1,128)S(1)}, s32[8,12,1]{1,2,0:T(1,128)}, u32[]{:S(2)}) copy-start(s32[8,12,1]{1,2,0:T(1,128)} %param.21) | copy-start | bytes 1156
  15.1 2.7 %copy-start = (bf16[1024,1024]{1,0:T(8,128)(2,1)S(1)}, bf16[1024,1024]{1,0:T(8,128)(2,1)}, u32[]{:S(2)}) copy-start(bf16[1024,1024]{1,0:T(8,128)(2,1)} %tab_ref.1) | copy-start | bytes 6291460
  15.7 36.3 %copy-start.10 = (s32[8]{0:T(128)S(1)}, s32[8]{0:T(128)}, u32[]{:S(2)}) copy-start(s32[8]{0:T(128)} %param.23) | copy-start | bytes 100
  52.0 3.8 %copy-start.1 = (bf16[4,2,4,4,16,512]{5,4,3,2,1,0:T(8,128)(2,1)}, bf16[4,2,4,4,16,512]{5,4,3,2,1,0:T(8,128)(2,1)S(1)}, u32[]{:S(2)}) copy-start(bf16[4,2,4,4,16,512]{5,4,3,2,1,0:T(8,128)(2,1)S(1)} %get-tuple-element.14) | copy-start | bytes 6291460
  52.0 3.8 %copy-start.2 = (f32[4,2,4,4,8,128]{5,4,3,2,1,0:T(8,128)}, f32[4,2,4,4,8,128]{5,4,3,2,1,0:T(8,128)S(1)}, u32[]{:S(2)}) copy-start(f32[4,2,4,4,8,128]{5,4,3,2,1,0:T(8,128)S(1)} %get-tuple-element.15.idall) | copy-start | bytes 1572868
  54.3 1.4 copy-start.13
  55.7 10.2 %copy-start.3 = (bf16[1024,1024]{1,0:T(8,128)(2,1)}, bf16[1024,1024]{1,0:T(8,128)(2,1)S(1)}, u32[]{:S(2)}) copy-start(bf16[1024,1024]{1,0:T(8,128)(2,1)S(1)} %get-tuple-element.27) | copy-start | bytes 6291460
  87.1 5.9 %copy-start.4 = (bf16[1024,1024]{1,0:T(8,128)(2,1)S(1)}, bf16[1024,1024]{1,0:T(8,128)(2,1)}, u32[]{:S(2)}) copy-start(bf16[1024,1024]{1,0:T(8,128)(2,1)} %copy-done.3) | copy-start | bytes 6291460
  87.1 5.9 %copy-start.16 = (bf16[1024,2048]{1,0:T(8,128)(2,1)S(1)}, bf16[1024,2048]{1,0:T(8,128)(2,1)}, u32[]{:S(2)}) copy-start(bf16[1024,2048]{1,0:T(8,128)(2,1)} %copy-done.15) | copy-start | bytes 12582916

commit v2 on v1

v2 whole, which is shorter than its diff:
```python
import functools

import jax
import jax.numpy as jnp
from jax import lax
from jax.experimental import pallas as pl
from jax.experimental.pallas import tpu as pltpu
from jax.sharding import PartitionSpec as P

logit_divisor = 0.05
norm_eps = 1e-06
MESH = pl.DeviceIdType.MESH
F32, BF16 = jnp.float32, jnp.bfloat16
VMEM_BYTES = 60 * 1024 * 1024


def place():
    c, b = lax.axis_index("corpus"), lax.axis_index("batch")
    return c // 2, c % 2, b // 4, b % 4


def device(z, k, y, x):
    return (z * 2 + k, y * 4 + x)


def moved(here, dim, offset):
    z, k, y, x = here
    at = [z, y, x]
    at[dim] = lax.rem(at[dim] + offset, 4)
    return device(at[0], k, at[1], at[2]), at[dim]


def greet(peers):
    barrier = pltpu.get_barrier_semaphore()
    for peer in peers:
        pl.semaphore_signal(barrier, inc=1, device_id=peer, device_id_type=MESH)
    pl.semaphore_wait(barrier, len(peers))


def push(src, dst, send, recv, peer):
    copy = pltpu.make_async_remote_copy(
        src_ref=src, dst_ref=dst, send_sem=send, recv_sem=recv, device_id=peer, device_id_type=MESH
    )
    copy.start()
    return copy


PARTS = (((0, 384), (384, 768), (768, 1024)), ((0, 384), (384, 640), (640, 1024)))
ORDER = ((0, 1, 2), (1, 2, 0), (2, 0, 1))


def pick(ref, axis, index, columns=None):
    at = [slice(None)] * (len(ref.shape) - 2)
    at[axis] = index
    return ref.at[tuple(at) + (slice(None), slice(None) if columns is None else pl.ds(columns[0], columns[1] - columns[0]))]


def dot(a, b, ca=1, cb=0):
    return lax.dot_general(a, b, (((ca,), (cb,)), ((), ())), preferred_element_type=F32)


def step_kernel(
    tok_hbm, win_hbm, wout_hbm, tab_hbm, bias_in, bias_out, gain, shift, queries, q_half, ids_own, counts,
    g_in, g_bias_in, g_out, g_bias_out, g_gain, g_shift, g_table,
    tok, win, wout, tab, tab_own, tok_t, hidden, slope, normed, inv_std, d_sum, d_pre, bias_acc,
    qall, idall, qcol, idcol, dots, dall, turned,
    part, r0, r1, s1, r2, s2, r3, sm, cg,
    load, sems_q, semr_q, dsem, dsemr, sem0, rsem0, sems, semr, qs, qr, cs, cr,
):
    here = place()
    z, k, y, x = here
    coord = (z, y, x)
    c = z * 2 + k
    sibling = device(z, 1 - k, y, x)
    sent = []

    def local(src, dst, n):
        copy = pltpu.make_async_copy(src, dst, load.at[n])
        copy.start()
        return copy

    tok_in = local(tok_hbm, tok, 0)
    win_in = [local(win_hbm.at[:, pl.ds(512 * n, 512)], win.at[:, pl.ds(512 * n, 512)], 1 + n) for n in range(4)]
    tab_in = local(tab_hbm, tab, 5)
    wout_in = local(wout_hbm, wout, 6)
    own_in = local(tab_hbm.at[pl.ds(pl.multiple_of((y * 4 + x) * 64, 64), 64), :], tab_own, 7)

    column = []
    for j in range(4):
        for e in range(2):
            if j or e:
                column.append(device(lax.rem(z + j, 4), lax.rem(k + e, 2), y, x))
    greet(column + [moved(here, dim, j)[0] for dim in (1, 2) for j in (1, 2, 3)])

    qall[z, k, y, x] = q_half[...]
    idall[z, k, y, x] = ids_own[...]
    payload = ((0, qall), (1, idall))
    first = []
    for j in (1, 2, 3):
        peer, _ = moved(here, 0, j)
        for n, buf in payload:
            mine = buf.at[z, k, y, x]
            first.append(push(mine, mine, sems_q.at[0, n, j - 1], semr_q.at[0, n, j - 1], peer))

    def gather_second():
        for copy in first:
            copy.wait_recv()
        copies = []
        for n, buf, dst in ((0, qall, qcol), (1, idall, idcol)):
            copies.append(push(buf.at[:, k, y, x], dst.at[k], sems_q.at[1, n, 0], semr_q.at[1, n, 0], sibling))
        for j in (1, 2, 3):
            peer, _ = moved(here, 1, j)
            for n, buf in payload:
                mine = buf.at[:, k, y, x]
                copies.append(push(mine, mine, sems_q.at[2, n, j - 1], semr_q.at[2, n, j - 1], peer))
        qcol[k] = qall[:, k, y, x]
        idcol[k] = idall[:, k, y, x]
        return copies

    def gather_third():
        copies = []
        for j in (1, 2, 3):
            peer, _ = moved(here, 2, j)
            for n, buf in payload:
                mine = buf.at[:, k, :, x]
                copies.append(push(mine, mine, sems_q.at[3, n, j - 1], semr_q.at[3, n, j - 1], peer))
        return copies

    def gather_last():
        copies = []
        for n, buf in payload:
            mine = buf.at[:, k]
            copies.append(push(mine, mine, sems_q.at[4, n, 0], semr_q.at[4, n, 0], sibling))
        return copies

    def project(n, carry):
        at = pl.ds(pl.multiple_of(n * 256, 256), 256)
        weight = win[:, at]
        bias = bias_in[:, at]
        for m in range(4):
            rows = slice(m * 256, m * 256 + 256)
            pre = dot(tok[rows, :], weight) + bias
            cdf = 0.5 * (1.0 + lax.erf(pre * 0.7071067811865476))
            hidden[rows, at] = (pre * cdf).astype(BF16)
            slope[rows, at] = cdf + pre * 0.3989422804014327 * jnp.exp(-0.5 * pre * pre)
        turn = pl.ds(pl.multiple_of(n * 128, 128), 128)
        tok_t[turn, :] = tok[:, turn].T
        return carry

    tok_in.wait()
    win_in[0].wait()
    lax.fori_loop(0, 2, project, 0)
    second = gather_second()
    win_in[1].wait()
    lax.fori_loop(2, 4, project, 0)
    for copy in second:
        copy.wait_recv()
    third = gather_third()
    sent += first + second + third

    tab_in.wait()
    own_in.wait()
    wide_q = qcol[...].astype(F32).reshape(8, 16, 512)
    left = wide_q[:, :8].reshape(64, 512).astype(BF16)
    right = wide_q[:, 8:].reshape(64, 512).astype(BF16)
    ids = jnp.concatenate([idcol[...].reshape(64, 128), jnp.zeros((64, 128), F32)], axis=0).T[:16, :64]
    dots[...] = jnp.zeros_like(dots)

    def score_rows(i, carry):
        start = pl.multiple_of(i * 128, 128)
        block = tab[pl.ds(start, 128), :]
        wide = block.astype(F32)
        scale = lax.rsqrt(jnp.sum(wide * wide, axis=1, keepdims=True) + norm_eps)
        score = (dot(block[:, :512], left, 1, 1) + dot(block[:, 512:], right, 1, 1)) * scale
        names = (lax.broadcasted_iota(jnp.int32, (128, 64), 0) + (start + c * 1024)).astype(F32)
        found = []
        for slot in range(12):
            hit = jnp.where(names == ids[slot : slot + 1, :], score, 0.0)
            found.append(jnp.sum(hit, axis=0, keepdims=True))
        found.append(jnp.zeros((4, 64), F32))
        dots[:, :64] += jnp.concatenate(found, axis=0)
        return carry

    lax.fori_loop(0, 8, score_rows, 0)
    back = [push(dots, dall.at[n], dsem.at[n], dsemr.at[n], peer) for n, peer in enumerate(column)]
    sent += back

    win_in[2].wait()
    win_in[3].wait()
    lax.fori_loop(4, 8, project, 0)

    for copy in third:
        copy.wait_recv()
    last = gather_last()
    sent += last

    wout_in.wait()
    which = lax.broadcasted_iota(jnp.int32, (8, 1024), 0)

    def normalise(i, carry):
        rows = pl.ds(pl.multiple_of(i * 256, 256), 256)
        summed = tok[rows, :].astype(F32) + dot(hidden[rows, :], wout[...]) + bias_out[...]
        centred = summed - jnp.mean(summed, axis=1, keepdims=True)
        inv = lax.rsqrt(jnp.mean(centred * centred, axis=1, keepdims=True) + norm_eps)
        value = centred * inv
        normed[rows, :] = value
        inv_std[rows, :] = jnp.broadcast_to(inv, (256, 128))
        for h in range(2):
            line = jnp.sum(value[h * 128 : h * 128 + 128], axis=0, keepdims=True)
            carry = jnp.where(which == 2 * i + h, line, carry)
        return carry

    norm_sum = lax.fori_loop(0, 4, normalise, jnp.zeros((8, 1024), F32))

    for copy in back:
        copy.wait_recv()
    total = dots[...]
    for n in range(7):
        total += dall[n]
    turned[...] = jnp.concatenate([total, jnp.zeros((112, 128), F32)], axis=0).T
    raw = turned[pl.ds(pl.multiple_of((k * 4 + z) * 8, 8), 8), :]
    pooled = norm_sum * gain[...] + 128.0 * shift[...]
    emb_scale = lax.rsqrt(jnp.sum(pooled * pooled, axis=1, keepdims=True) + norm_eps)
    emb = pooled * emb_scale
    query = queries[...].astype(F32)
    q_scale = lax.rsqrt(jnp.sum(query * query, axis=1, keepdims=True) + norm_eps)
    question = query * q_scale
    positive = jnp.sum(question * emb, axis=1, keepdims=True) / logit_divisor
    live = lax.broadcasted_iota(jnp.int32, (8, 128), 1) < counts[...]
    weights = jnp.where(live, jnp.exp(raw * q_scale / logit_divisor), 0.0)
    own = jnp.exp(positive)
    whole = own + jnp.sum(weights, axis=1, keepdims=True)
    cg[z, k, y, x] = weights / whole / logit_divisor * q_scale
    emb_slope = ((own / whole - 1.0) / logit_divisor) * question
    d_pooled = emb_scale * (emb_slope - emb * jnp.sum(emb * emb_slope, axis=1, keepdims=True))
    grad_shift = jnp.sum(d_pooled, axis=0, keepdims=True) * 128.0
    grad_gain = jnp.sum(d_pooled * norm_sum, axis=0, keepdims=True)
    lead = d_pooled * gain[...]

    def slopes(step):
        if step == 0:
            mine = cg.at[z, k, y, x]
            return [push(mine, mine, cs.at[0, 0], cr.at[0, 0], sibling)]
        dim = step - 1
        every = slice(None)
        mine = cg.at[((z, every, y, x), (every, every, y, x), (every, every, every, x))[dim]]
        copies = []
        for j in (1, 2, 3):
            peer, _ = moved(here, dim, j)
            copies.append(push(mine, mine, cs.at[step, j - 1], cr.at[step, j - 1], peer))
        return copies

    def arrived(copies):
        for copy in copies:
            copy.wait_recv()

    slope_step = slopes(0)
    sent += slope_step

    def back_norm(i, carry):
        rows = pl.ds(pl.multiple_of(i * 128, 128), 128)
        g = jnp.sum(jnp.where(which == i, lead, 0.0), axis=0, keepdims=True)
        value = normed[rows, :]
        inv = inv_std[rows, :][:, :1]
        both = jnp.mean(value * g, axis=1, keepdims=True)
        ds = inv * (g - jnp.mean(g, axis=1, keepdims=True) - value * both)
        d_sum[rows, :] = ds.astype(BF16)
        return carry + jnp.sum(ds, axis=0, keepdims=True)

    grad_bias_out = lax.fori_loop(0, 8, back_norm, jnp.zeros((1, 1024), F32))
    arrived(slope_step)
    slope_step = slopes(1)
    sent += slope_step

    def grad_out(zz, core):
        at = pl.ds(pl.multiple_of((zz * 2 + core) * 256, 256), 256)
        value = dot(hidden[:, at], d_sum[...], 0, 0)
        part[0, zz, core] = value.astype(BF16).reshape(4, 4, 16, 1024)

    zero = {}
    for zz in range(4):
        grad_out(zz, 1 - k)
        zero[0, zz] = push(part.at[0, zz, 1 - k], r0.at[0, zz], sem0.at[0, zz], rsem0.at[0, zz], sibling)

    def own_blocks(zz, carry):
        grad_out(zz, k)
        return carry

    lax.fori_loop(0, 4, own_blocks, 0)
    arrived(slope_step)
    slope_step = slopes(2)
    sent += slope_step

    def add_core(w, lo, hi, first, last):
        def one(i, carry):
            a, e, f = i // 16, lax.rem(i // 4, 4), lax.rem(i, 4)
            r0[w, a, e, f, :, lo:hi] = (
                r0[w, a, e, f, :, lo:hi].astype(F32) + part[w, a, k, e, f, :, lo:hi].astype(F32)
            ).astype(BF16)
            return carry
        lax.fori_loop(first, last, one, 0)

    def stage_one(w, p):
        dim = ORDER[p][0]
        copies = []
        for j in (1, 2, 3):
            peer, to = moved(here, dim, j)
            src = pick(r0.at[w], dim, to, PARTS[w][p])
            copies.append(push(src, r1[w][p].at[j - 1], sems.at[0, w, p, j - 1], semr.at[0, w, p, j - 1], peer))
        return copies

    def add_one(w, p):
        dim = ORDER[p][0]
        mine = pick(r0.at[w], dim, coord[dim], PARTS[w][p])

        def one(i, carry):
            e, f = i // 4, lax.rem(i, 4)
            value = mine[e, f].astype(F32)
            for j in range(3):
                value += r1[w][p][j, e, f].astype(F32)
            s1[w][p][e, f] = value.astype(BF16)
            return carry
        lax.fori_loop(0, 16, one, 0)

    def stage_two(w, p):
        dim = ORDER[p][1]
        rest = [d for d in (0, 1, 2) if d != ORDER[p][0]]
        copies = []
        for j in (1, 2, 3):
            peer, to = moved(here, dim, j)
            src = pick(s1[w][p], rest.index(dim), to)
            copies.append(push(src, r2[w][p].at[j - 1], sems.at[1, w, p, j - 1], semr.at[1, w, p, j - 1], peer))
        return copies

    def add_two(w, p):
        dim = ORDER[p][1]
        rest = [d for d in (0, 1, 2) if d != ORDER[p][0]]
        mine = pick(s1[w][p], rest.index(dim), coord[dim])
        for e in range(4):
            value = mine[e].astype(F32)
            for j in range(3):
                value += r2[w][p][j, e].astype(F32)
            s2[w][p][e] = value

    def stage_three(w, p):
        dim = ORDER[p][2]
        copies = []
        for j in (1, 2, 3):
            peer, to = moved(here, dim, j)
            copies.append(push(s2[w][p].at[to], r3[w][p].at[j - 1], sems.at[2, w, p, j - 1], semr.at[2, w, p, j - 1], peer))
        return copies

    def add_three(w, p):
        lo, hi = PARTS[w][p]
        value = s2[w][p][coord[ORDER[p][2]]]
        for j in range(3):
            value += r3[w][p][j]
        if w == 0:
            g_out[:, lo:hi] = value
        else:
            for n in range((hi - lo) // 128):
                tile = value[:, n * 128 : n * 128 + 128]
                g_in[:, 2 * lo + 256 * n : 2 * lo + 256 * n + 128] = tile[:8]
                g_in[:, 2 * lo + 256 * n + 128 : 2 * lo + 256 * n + 256] = tile[8:]

    def back_layer(n, carry):
        at = pl.ds(pl.multiple_of(n * 256, 256), 256)
        weight = wout[at, :]
        line = jnp.zeros((1, 256), F32)
        for m in range(4):
            rows = slice(m * 256, m * 256 + 256)
            value = dot(d_sum[rows, :], weight, 1, 1) * slope[rows, at]
            line += jnp.sum(value, axis=0, keepdims=True)
            d_pre[rows, :] = value.astype(BF16)
        bias_acc[:, at] = line
        to = pl.ds(pl.multiple_of(n * 128, 128), 128)
        for m in range(4):
            value = dot(tok_t[m * 256 : m * 256 + 256, :], d_pre[...])
            value = value.reshape(32, 8, 256)
            value = jnp.concatenate([value[:, :, :128], value[:, :, 128:]], axis=1).astype(BF16)
            part[1, m, :, :, :, :, to] = value.reshape(2, 4, 4, 16, 128)
        return carry

    ones, twos, threes = {}, {}, {}

    def run_part(p):
        lo, hi = PARTS[1][p]
        lax.fori_loop(lo // 128, hi // 128, back_layer, 0)
        cut = pl.ds(lo, hi - lo)
        zero[1, p] = push(
            part.at[1, :, 1 - k, :, :, :, cut], r0.at[1, :, :, :, :, cut], sem0.at[1, p], rsem0.at[1, p], sibling
        )

    run_part(0)
    for zz in range(4):
        zero[0, zz].wait_recv()
        add_core(0, 0, 1024, 16 * zz, 16 * zz + 16)
    for p in range(3):
        ones[0, p] = stage_one(0, p)
    arrived(slope_step)
    slope_step = slopes(3)
    sent += slope_step

    def finish_core(p):
        zero[1, p].wait_recv()
        add_core(1, PARTS[1][p][0], PARTS[1][p][1], 0, 64)
        ones[1, p] = stage_one(1, p)

    run_part(1)
    finish_core(0)
    run_part(2)
    finish_core(1)

    sm[0, k] = jnp.concatenate(
        [bias_acc[:, :1024], bias_acc[:, 1024:], grad_bias_out, grad_gain, grad_shift, jnp.zeros((3, 1024), F32)], axis=0
    )
    small = [push(sm.at[0, k], sm.at[0, k], qs.at[0, 0], qr.at[0, 0], sibling)]
    sent += small

    def stage_small(step):
        dim = step - 1
        got = sm[step - 1, 0] + sm[step - 1, 1]
        if step > 1:
            got = (got + sm[step - 1, 2]) + sm[step - 1, 3]
        sm[step, coord[dim]] = got
        copies = []
        for j in (1, 2, 3):
            peer, _ = moved(here, dim, j)
            mine = sm.at[step, coord[dim]]
            copies.append(push(mine, mine, qs.at[step, j - 1], qr.at[step, j - 1], peer))
        return copies

    def second_stage(w, p):
        arrived(ones[w, p])
        add_one(w, p)
        twos[w, p] = stage_two(w, p)

    def third_stage(w, p):
        arrived(twos[w, p])
        add_two(w, p)
        threes[w, p] = stage_three(w, p)

    def end_stage(w, p):
        arrived(threes[w, p])
        add_three(w, p)

    for p in range(3):
        second_stage(0, p)
    finish_core(2)
    arrived(small)
    small = stage_small(1)
    sent += small
    arrived(slope_step)
    arrived(last)

    base = c * 1024 + (y * 4 + x) * 64
    row = (lax.broadcasted_iota(jnp.int32, (256, 128), 1) + base).astype(F32)

    def collect(i, carry):
        name, value = idall[i].reshape(256, 128), cg[i].reshape(256, 128)
        weight = jnp.zeros((256, 128), F32)
        for slot in range(12):
            weight += jnp.where(name[:, slot : slot + 1] == row, value[:, slot : slot + 1], 0.0)
        high = weight.astype(BF16)
        low = (weight - high.astype(F32)).astype(BF16)
        some = qall[i].astype(F32).reshape(32, 16, 512)
        halves = []
        for h in range(2):
            half = some[:, h * 8 : h * 8 + 8].reshape(256, 512).astype(BF16)
            halves.append(dot(high, half, 0, 0) + dot(low, half, 0, 0))
        return tuple(a + b[:64] for a, b in zip(carry, halves))

    sums = lax.fori_loop(0, 4, collect, (jnp.zeros((64, 512), F32),) * 2)
    table_slope = jnp.concatenate(sums, axis=1)
    rows = tab_own[...].astype(F32)
    scale = lax.rsqrt(jnp.sum(rows * rows, axis=1, keepdims=True) + norm_eps)
    unit = rows * scale
    g_table[...] = scale * (table_slope - unit * jnp.sum(unit * table_slope, axis=1, keepdims=True))

    for p in range(3):
        third_stage(0, p)
    arrived(small)
    small = stage_small(2)
    sent += small
    for p in range(3):
        second_stage(1, p)
    arrived(small)
    small = stage_small(3)
    sent += small
    for p in range(3):
        end_stage(0, p)
    for p in range(3):
        third_stage(1, p)
    arrived(small)
    got = ((sm[3, 0] + sm[3, 1]) + sm[3, 2]) + sm[3, 3]
    g_bias_in[:, :1024] = got[0:1]
    g_bias_in[:, 1024:] = got[1:2]
    g_bias_out[...] = got[2:3]
    g_gain[...] = got[3:4]
    g_shift[...] = got[4:5]
    for p in range(3):
        end_stage(1, p)
    for group in (ones, twos, threes):
        for copies in group.values():
            sent += copies
    for copy in sent + list(zero.values()):
        copy.wait_send()


def step(*operands):
    vmem, hbm = pl.BlockSpec(memory_space=pltpu.VMEM), pl.BlockSpec(memory_space=pl.ANY)

    def scratch(shape, kind):
        return tuple(tuple(pltpu.VMEM(shape + (16, hi - lo), kind) for lo, hi in row) for row in PARTS)

    dma = pltpu.SemaphoreType.DMA
    out = jax.ShapeDtypeStruct
    return pl.pallas_call(
        step_kernel,
        out_shape=(
            out((8, 2048), F32),
            out((1, 2048), F32),
            out((16, 1024), F32),
            out((1, 1024), F32),
            out((1, 1024), F32),
            out((1, 1024), F32),
            out((64, 1024), F32),
        ),
        in_specs=[hbm] * 4 + [vmem] * 8,
        out_specs=(vmem,) * 7,
        scratch_shapes=[
            pltpu.VMEM((1024, 1024), BF16),
            pltpu.VMEM((1024, 2048), BF16),
            pltpu.VMEM((2048, 1024), BF16),
            pltpu.VMEM((1024, 1024), BF16),
            pltpu.VMEM((64, 1024), BF16),
            pltpu.VMEM((1024, 1024), BF16),
            pltpu.VMEM((1024, 2048), BF16),
            pltpu.VMEM((1024, 2048), F32),
            pltpu.VMEM((1024, 1024), F32),
            pltpu.VMEM((1024, 128), F32),
            pltpu.VMEM((1024, 1024), BF16),
            pltpu.VMEM((1024, 256), BF16),
            pltpu.VMEM((1, 2048), F32),
            pltpu.VMEM((4, 2, 4, 4, 16, 512), BF16),
            pltpu.VMEM((4, 2, 4, 4, 8, 128), F32),
            pltpu.VMEM((2, 4, 16, 512), BF16),
            pltpu.VMEM((2, 4, 8, 128), F32),
            pltpu.VMEM((16, 128), F32),
            pltpu.VMEM((7, 16, 128), F32),
            pltpu.VMEM((128, 128), F32),
            pltpu.VMEM((2, 4, 2, 4, 4, 16, 1024), BF16),
            pltpu.VMEM((2, 4, 4, 4, 16, 1024), BF16),
            scratch((3, 4, 4), BF16),
            scratch((4, 4), BF16),
            scratch((3, 4), BF16),
            scratch((4,), F32),
            scratch((3,), F32),
            pltpu.VMEM((4, 4, 8, 1024), F32),
            pltpu.VMEM((4, 2, 4, 4, 8, 128), F32),
            dma((8,)),
            dma((5, 2, 3)),
            dma((5, 2, 3)),
            dma((7,)),
            dma((7,)),
            dma((2, 4)),
            dma((2, 4)),
            dma((3, 2, 3, 3)),
            dma((3, 2, 3, 3)),
            dma((4, 3)),
            dma((4, 3)),
            dma((4, 3)),
            dma((4, 3)),
        ],
        compiler_params=pltpu.CompilerParams(
            collective_id=0, has_side_effects=True, vmem_limit_bytes=VMEM_BYTES
        ),
    )(*operands)


def body(
    tokens,
    weight_in,
    bias_in,
    weight_out,
    bias_out,
    norm_gain,
    norm_shift,
    queries,
    corpus_table,
    neg_owner,
    neg_row,
    neg_count,
):
    count_q, seq, width = tokens.shape
    slots = neg_row.shape[1]
    ids = (neg_owner.reshape(count_q, slots) * 1024 + neg_row).astype(F32)
    ids = jnp.pad(ids, ((0, 0), (0, 128 - slots)), constant_values=-1.0)
    q_half = jnp.concatenate([queries[:, :512], queries[:, 512:]], axis=0)
    counts = jnp.broadcast_to(neg_count[:, None], (count_q, 128))
    grad_in, g_bias_in, grad_out, g_bias_out, g_gain, g_shift, grad_table = step(
        tokens.reshape(count_q * seq, width),
        weight_in,
        weight_out,
        corpus_table,
        bias_in[None],
        bias_out[None],
        norm_gain[None],
        norm_shift[None],
        queries,
        q_half,
        ids,
        counts,
    )
    return (grad_in, g_bias_in[0], grad_out, g_bias_out[0], g_gain[0], g_shift[0], grad_table)


def solution(mesh):
    return jax.shard_map(
        body,
        mesh=mesh,
        in_specs=(
            P(("corpus", "batch"), None, None),
            P(),
            P(),
            P(),
            P(),
            P(),
            P(),
            P(("corpus", "batch"), None),
            P("corpus", None),
            P(("corpus", "batch"), None, None),
            P(("corpus", "batch"), None),
            P(("corpus", "batch")),
        ),
        out_specs=(
            P(("corpus", "batch"), None),
            P(),
            P(("corpus", "batch"), None),
            P(),
            P(),
            P(),
            P(("corpus", "batch"), None),
        ),
        check_vma=False,
    )
```

time: 168 us -> 103 us (0.61)
  matrix products: 37 us -> 0 us
  local copies, waits for them, and re-layouts: 27.7 us -> 12.4 us
  other arithmetic: 13.5 us -> 1.32 us
    dot_general x5 -> x0, matrix products: 37 us -> none  [the longest x1 10.2 us: body(): lax.dot_general(d_sum_low, weight_out, (((1,), (1,)), ((), ())), preferre...]
    convert_element_type x3 -> x0, local copies, waits for them, and re-layouts: 20.2 us -> none  [body(): part_in.reshape(128, 8, 2, 1024).transpose(0, 2, 1, 3).astype(BF16)]
    unnamed x35 -> x7, local copies, waits for them, and re-layouts: 1.8 us -> 9.73 us
    another operation x1 -> x0, other arithmetic: 7.62 us -> none  [body(): jnp.stack([part_out.reshape(128, 16, 1024), part_in.reshape(128, 16, 1024)])]
    reduce_sum x11 -> x0, other arithmetic: 5.13 us -> none  [the longest x1 1.53 us: body(): jnp.sum(normed.reshape(count_q, seq, width), axis=1)]
    slice x2 -> x0, local copies, waits for them, and re-layouts: 2.59 us -> none  [the longest x1 1.29 us: body(): small[:2048]]
    pallas_call x2 -> x1, Pallas kernels: 88.2 us -> 88.1 us  [step(): pl.pallas_call(step_kernel, out_shape=(out((8, 2048), F32), out((1, 2048)...]
where the time goes in v2:
time: 103 us; the launch traced here: 102 us
  Pallas kernels  88.1 us (86%)
  local copies, waits for them, and re-layouts  12.4 us (12%)
  other arithmetic  1.32 us (1%)
    pallas_call x1, Pallas kernels, step(): pl.pallas_call(step_kernel, out_shape=(out((8, 2048), F32), out((1, 2048)...  88.1 us
    unnamed x7, local copies, waits for them, and re-layouts  9.73 us

profile of v2, /device:TPU:0, one launch (start us, length us, event | category | flops | bytes accessed | tf_op | source)
XLA Modules:
  0.0 102.4 jit_solution(2601775848123381077)
XLA Ops:
  0.6 0.7 fusion
  1.3 0.6 pad.4.ids_own
  1.9 1.3 %broadcast_in_dim.22.counts = s32[8,128]{1,0:T(8,128)} broadcast(s32[8]{0:T(128)} %param.23), dimensions={0} | broadcast | bytes 4128 | tf_op jit(solution)/shard_map/broadcast_in_dim | solution.py:600
  3.3 0.7 fusion.1
  4.0 0.6 pad_maximum_fusion.q_half
  4.6 88.1 %shard_map.171 = (f32[8,2048]{1,0:T(8,128)}, f32[1,2048]{1,0:T(1,128)}, f32[16,1024]{1,0:T(8,128)}, f32[1,1024]{1,0:T(1,128)}, f32[1,1024]{1,0:T(1,128)}, /*index=5*/f32[1,1024]{1,0:T(1,128)}, f32[64,1024]{1,0:T(8,128)}) custom-call(bf16[1024,1024]{1,0:T(8,128)(2,1)} %bitcast.14, bf16[1024,2048]{1,0:T(8,128)(2,1)} %win_hbm.1, bf16[2048,1024]{1,0:T(8,128)(2,1)} %wout_hbm.1, ...), custom_call_target="tpu_custom_call" | custom-call | tf_op jit(solution)/shard_map/pallas_call | solution.py:518
  92.7 1.5 %copy.27 = f32[8,2048]{1,0:T(8,128)} copy(f32[8,2048]{1,0:T(8,128)} %get-tuple-element.30) | data formatting | bytes 131072
  94.1 1.3 %copy.28 = f32[2048]{0:T(1024)} copy(f32[2048]{0:T(1024)} %bitcast.16) | data formatting | bytes 16384
  95.4 1.5 %copy.29 = f32[16,1024]{1,0:T(8,128)} copy(f32[16,1024]{1,0:T(8,128)} %get-tuple-element.32) | data formatting | bytes 131072
  96.9 1.3 %copy.30 = f32[1024]{0:T(1024)} copy(f32[1024]{0:T(1024)} %bitcast.23) | data formatting | bytes 8192
  98.2 1.3 %copy.31 = f32[1024]{0:T(1024)} copy(f32[1024]{0:T(1024)} %bitcast.22) | data formatting | bytes 8192
  99.5 1.3 %copy.32 = f32[1024]{0:T(1024)} copy(f32[1024]{0:T(1024)} %bitcast.21) | data formatting | bytes 8192
  100.7 1.7 %copy.33 = f32[64,1024]{1,0:T(8,128)} copy(f32[64,1024]{1,0:T(8,128)} %get-tuple-element.36) | data formatting | bytes 524288

commit v3 on v2

--- a/solution.py
+++ b/solution.py
@@ -30,6 +30,13 @@
     return device(at[0], k, at[1], at[2]), at[dim]
 
 
+def put(here, dim, to):
+    z, k, y, x = here
+    at = [z, y, x]
+    at[dim] = to
+    return device(at[0], k, at[1], at[2])
+
+
 def greet(peers):
     barrier = pltpu.get_barrier_semaphore()
     for peer in peers:
@@ -60,11 +67,11 @@
 
 
 def step_kernel(
-    tok_hbm, win_hbm, wout_hbm, tab_hbm, bias_in, bias_out, gain, shift, queries, q_half, ids_own, counts,
+    tok_hbm, win_hbm, wout_hbm, tab_hbm, bias_in, bias_out, gain, shift, queries, slot,
     g_in, g_bias_in, g_out, g_bias_out, g_gain, g_shift, g_table,
     tok, win, wout, tab, tab_own, tok_t, hidden, slope, normed, inv_std, d_sum, d_pre, bias_acc,
     qall, idall, qcol, idcol, dots, dall, turned,
-    part, r0, r1, s1, r2, s2, r3, sm, cg,
+    part, r0, r1, s1, r2, t2, s2, r3, sm, cg,
     load, sems_q, semr_q, dsem, dsemr, sem0, rsem0, sems, semr, qs, qr, cs, cr,
 ):
     here = place()
@@ -72,6 +79,9 @@
     coord = (z, y, x)
     c = z * 2 + k
     sibling = device(z, 1 - k, y, x)
+    fst = [(1 - k) * (i + 1 - 2 * lax.rem(i, 2)) + k * (3 - i) for i in coord]
+    snd = [k * (i + 1 - 2 * lax.rem(i, 2)) + (1 - k) * (3 - i) for i in coord]
+    opp = [lax.rem(i + 2, 4) for i in coord]
     sent = []
 
     def local(src, dst, n):
@@ -92,8 +102,10 @@
                 column.append(device(lax.rem(z + j, 4), lax.rem(k + e, 2), y, x))
     greet(column + [moved(here, dim, j)[0] for dim in (1, 2) for j in (1, 2, 3)])
 
-    qall[z, k, y, x] = q_half[...]
-    idall[z, k, y, x] = ids_own[...]
+    query = queries[...].astype(F32)
+    qall[z, k, y, x] = jnp.concatenate([query[:, :512], query[:, 512:]], axis=0).astype(BF16)
+    lane = lax.broadcasted_iota(jnp.int32, (8, 128), 1)
+    idall[z, k, y, x] = jnp.where(lane < 12, slot[...], -1.0)
     payload = ((0, qall), (1, idall))
     first = []
     for j in (1, 2, 3):
@@ -119,11 +131,19 @@
 
     def gather_third():
         copies = []
-        for j in (1, 2, 3):
-            peer, _ = moved(here, 2, j)
+        for m, to in enumerate((fst[2], snd[2])):
             for n, buf in payload:
                 mine = buf.at[:, k, :, x]
-                copies.append(push(mine, mine, sems_q.at[3, n, j - 1], semr_q.at[3, n, j - 1], peer))
+                copies.append(push(mine, mine, sems_q.at[3, n, m], semr_q.at[3, n, m], put(here, 2, to)))
+        return copies
+
+    def gather_fourth():
+        for copy in third[:2]:
+            copy.wait_recv()
+        copies = []
+        for n, buf in payload:
+            near = buf.at[:, k, :, fst[2]]
+            copies.append(push(near, near, sems_q.at[3, n, 2], semr_q.at[3, n, 2], put(here, 2, snd[2])))
         return copies
 
     def gather_last():
@@ -189,10 +209,8 @@
     win_in[3].wait()
     lax.fori_loop(4, 8, project, 0)
 
-    for copy in third:
-        copy.wait_recv()
-    last = gather_last()
-    sent += last
+    fourth = gather_fourth()
+    sent += fourth
 
     wout_in.wait()
     which = lax.broadcasted_iota(jnp.int32, (8, 1024), 0)
@@ -222,11 +240,10 @@
     pooled = norm_sum * gain[...] + 128.0 * shift[...]
     emb_scale = lax.rsqrt(jnp.sum(pooled * pooled, axis=1, keepdims=True) + norm_eps)
     emb = pooled * emb_scale
-    query = queries[...].astype(F32)
     q_scale = lax.rsqrt(jnp.sum(query * query, axis=1, keepdims=True) + norm_eps)
     question = query * q_scale
     positive = jnp.sum(question * emb, axis=1, keepdims=True) / logit_divisor
-    live = lax.broadcasted_iota(jnp.int32, (8, 128), 1) < counts[...]
+    live = lane.astype(F32) < slot[:, 12:13]
     weights = jnp.where(live, jnp.exp(raw * q_scale / logit_divisor), 0.0)
     own = jnp.exp(positive)
     whole = own + jnp.sum(weights, axis=1, keepdims=True)
@@ -268,6 +285,10 @@
         return carry + jnp.sum(ds, axis=0, keepdims=True)
 
     grad_bias_out = lax.fori_loop(0, 8, back_norm, jnp.zeros((1, 1024), F32))
+    for copy in third[2:] + fourth:
+        copy.wait_recv()
+    last = gather_last()
+    sent += last
     arrived(slope_step)
     slope_step = slopes(1)
     sent += slope_step
@@ -300,14 +321,35 @@
             return carry
         lax.fori_loop(first, last, one, 0)
 
+    def swap(dim, w, p, step, near, far, land):
+        peer = put(here, dim, fst[dim])
+        return [
+            push(far, land[0], sems.at[step, w, p, 0], semr.at[step, w, p, 0], peer),
+            push(near, land[1], sems.at[step, w, p, 1], semr.at[step, w, p, 1], peer),
+        ]
+
+    def relay(dim, w, p, step, src, land):
+        return [push(src, land, sems.at[step, w, p, 2], semr.at[step, w, p, 2], put(here, dim, snd[dim]))]
+
+    def rest(p):
+        return [d for d in (0, 1, 2) if d != ORDER[p][0]]
+
     def stage_one(w, p):
         dim = ORDER[p][0]
-        copies = []
-        for j in (1, 2, 3):
-            peer, to = moved(here, dim, j)
-            src = pick(r0.at[w], dim, to, PARTS[w][p])
-            copies.append(push(src, r1[w][p].at[j - 1], sems.at[0, w, p, j - 1], semr.at[0, w, p, j - 1], peer))
-        return copies
+        cut = PARTS[w][p]
+        near, far = pick(r0.at[w], dim, fst[dim], cut), pick(r0.at[w], dim, opp[dim], cut)
+        return swap(dim, w, p, 0, near, far, (r1[w][p].at[0], r1[w][p].at[1]))
+
+    def relay_one(w, p):
+        dim = ORDER[p][0]
+        mine = pick(r0.at[w], dim, snd[dim], PARTS[w][p])
+
+        def one(i, carry):
+            e, f = i // 4, lax.rem(i, 4)
+            mine[e, f] = (mine[e, f].astype(F32) + r1[w][p][0, e, f].astype(F32)).astype(BF16)
+            return carry
+        lax.fori_loop(0, 16, one, 0)
+        return relay(dim, w, p, 0, mine, r1[w][p].at[2])
 
     def add_one(w, p):
         dim = ORDER[p][0]
@@ -315,46 +357,42 @@
 
         def one(i, carry):
             e, f = i // 4, lax.rem(i, 4)
-            value = mine[e, f].astype(F32)
-            for j in range(3):
-                value += r1[w][p][j, e, f].astype(F32)
+            value = mine[e, f].astype(F32) + r1[w][p][1, e, f].astype(F32) + r1[w][p][2, e, f].astype(F32)
             s1[w][p][e, f] = value.astype(BF16)
             return carry
         lax.fori_loop(0, 16, one, 0)
 
     def stage_two(w, p):
         dim = ORDER[p][1]
-        rest = [d for d in (0, 1, 2) if d != ORDER[p][0]]
-        copies = []
-        for j in (1, 2, 3):
-            peer, to = moved(here, dim, j)
-            src = pick(s1[w][p], rest.index(dim), to)
-            copies.append(push(src, r2[w][p].at[j - 1], sems.at[1, w, p, j - 1], semr.at[1, w, p, j - 1], peer))
-        return copies
+        axis = rest(p).index(dim)
+        near, far = pick(s1[w][p], axis, fst[dim]), pick(s1[w][p], axis, opp[dim])
+        return swap(dim, w, p, 1, near, far, (r2[w][p].at[0], r2[w][p].at[1]))
+
+    def relay_two(w, p):
+        dim = ORDER[p][1]
+        mine = pick(s1[w][p], rest(p).index(dim), snd[dim])
+        for e in range(4):
+            t2[w][p][0, e] = mine[e].astype(F32) + r2[w][p][0, e].astype(F32)
+        return relay(dim, w, p, 1, t2[w][p].at[0], t2[w][p].at[1])
 
     def add_two(w, p):
         dim = ORDER[p][1]
-        rest = [d for d in (0, 1, 2) if d != ORDER[p][0]]
-        mine = pick(s1[w][p], rest.index(dim), coord[dim])
+        mine = pick(s1[w][p], rest(p).index(dim), coord[dim])
         for e in range(4):
-            value = mine[e].astype(F32)
-            for j in range(3):
-                value += r2[w][p][j, e].astype(F32)
-            s2[w][p][e] = value
+            s2[w][p][e] = mine[e].astype(F32) + r2[w][p][1, e].astype(F32) + t2[w][p][1, e]
 
     def stage_three(w, p):
         dim = ORDER[p][2]
-        copies = []
-        for j in (1, 2, 3):
-            peer, to = moved(here, dim, j)
-            copies.append(push(s2[w][p].at[to], r3[w][p].at[j - 1], sems.at[2, w, p, j - 1], semr.at[2, w, p, j - 1], peer))
-        return copies
+        return swap(dim, w, p, 2, s2[w][p].at[fst[dim]], s2[w][p].at[opp[dim]], (r3[w][p].at[0], r3[w][p].at[1]))
+
+    def relay_three(w, p):
+        dim = ORDER[p][2]
+        s2[w][p][snd[dim]] += r3[w][p][0]
+        return relay(dim, w, p, 2, s2[w][p].at[snd[dim]], r3[w][p].at[2])
 
     def add_three(w, p):
         lo, hi = PARTS[w][p]
-        value = s2[w][p][coord[ORDER[p][2]]]
-        for j in range(3):
-            value += r3[w][p][j]
+        value = s2[w][p][coord[ORDER[p][2]]] + r3[w][p][1] + r3[w][p][2]
         if w == 0:
             g_out[:, lo:hi] = value
         else:
@@ -382,6 +420,21 @@
         return carry
 
     ones, twos, threes = {}, {}, {}
+    groups = (ones, twos, threes)
+
+    def start(step, w, p):
+        groups[step][w, p] = (stage_one, stage_two, stage_three)[step](w, p)
+
+    def pass_on(step, w, p):
+        groups[step][w, p][0].wait_recv()
+        groups[step][w, p] += (relay_one, relay_two, relay_three)[step](w, p)
+
+    def end(step, w, p):
+        for copy in groups[step][w, p][1:]:
+            copy.wait_recv()
+        (add_one, add_two, add_three)[step](w, p)
+        if step < 2:
+            start(step + 1, w, p)
 
     def run_part(p):
         lo, hi = PARTS[1][p]
@@ -391,25 +444,31 @@
             part.at[1, :, 1 - k, :, :, :, cut], r0.at[1, :, :, :, :, cut], sem0.at[1, p], rsem0.at[1, p], sibling
         )
 
-    run_part(0)
+    def finish_core(p):
+        zero[1, p].wait_recv()
+        add_core(1, PARTS[1][p][0], PARTS[1][p][1], 0, 64)
+        start(0, 1, p)
+
     for zz in range(4):
         zero[0, zz].wait_recv()
         add_core(0, 0, 1024, 16 * zz, 16 * zz + 16)
     for p in range(3):
-        ones[0, p] = stage_one(0, p)
+        start(0, 0, p)
+    run_part(0)
+    for p in range(3):
+        pass_on(0, 0, p)
     arrived(slope_step)
     slope_step = slopes(3)
     sent += slope_step
-
-    def finish_core(p):
-        zero[1, p].wait_recv()
-        add_core(1, PARTS[1][p][0], PARTS[1][p][1], 0, 64)
-        ones[1, p] = stage_one(1, p)
-
     run_part(1)
     finish_core(0)
+    for p in range(3):
+        end(0, 0, p)
     run_part(2)
     finish_core(1)
+    pass_on(0, 1, 0)
+    for p in range(3):
+        pass_on(1, 0, p)
 
     sm[0, k] = jnp.concatenate(
         [bias_acc[:, :1024], bias_acc[:, 1024:], grad_bias_out, grad_gain, grad_shift, jnp.zeros((3, 1024), F32)], axis=0
@@ -430,28 +489,21 @@
             copies.append(push(mine, mine, qs.at[step, j - 1], qr.at[step, j - 1], peer))
         return copies
 
-    def second_stage(w, p):
-        arrived(ones[w, p])
-        add_one(w, p)
-        twos[w, p] = stage_two(w, p)
-
-    def third_stage(w, p):
-        arrived(twos[w, p])
-        add_two(w, p)
-        threes[w, p] = stage_three(w, p)
-
-    def end_stage(w, p):
-        arrived(threes[w, p])
-        add_three(w, p)
-
+    finish_core(2)
+    pass_on(0, 1, 1)
+    end(0, 1, 0)
     for p in range(3):
-        second_stage(0, p)
-    finish_core(2)
+        end(1, 0, p)
     arrived(small)
     small = stage_small(1)
     sent += small
     arrived(slope_step)
     arrived(last)
+    pass_on(0, 1, 2)
+    end(0, 1, 1)
+    pass_on(1, 1, 0)
+    for p in range(3):
+        pass_on(2, 0, p)
 
     base = c * 1024 + (y * 4 + x) * 64
     row = (lax.broadcasted_iota(jnp.int32, (256, 128), 1) + base).astype(F32)
@@ -477,20 +529,23 @@
     unit = rows * scale
     g_table[...] = scale * (table_slope - unit * jnp.sum(unit * table_slope, axis=1, keepdims=True))
 
-    for p in range(3):
-        third_stage(0, p)
+    end(0, 1, 2)
+    pass_on(1, 1, 1)
     arrived(small)
     small = stage_small(2)
     sent += small
+    end(1, 1, 0)
+    pass_on(1, 1, 2)
     for p in range(3):
-        second_stage(1, p)
+        end(2, 0, p)
+    end(1, 1, 1)
+    pass_on(2, 1, 0)
     arrived(small)
     small = stage_small(3)
     sent += small
-    for p in range(3):
-        end_stage(0, p)
-    for p in range(3):
-        third_stage(1, p)
+    end(1, 1, 2)
+    pass_on(2, 1, 1)
+    pass_on(2, 1, 2)
     arrived(small)
     got = ((sm[3, 0] + sm[3, 1]) + sm[3, 2]) + sm[3, 3]
     g_bias_in[:, :1024] = got[0:1]
@@ -499,12 +554,27 @@
     g_gain[...] = got[3:4]
     g_shift[...] = got[4:5]
     for p in range(3):
-        end_stage(1, p)
-    for group in (ones, twos, threes):
+        end(2, 1, p)
+    for group in groups:
         for copies in group.values():
             sent += copies
     for copy in sent + list(zero.values()):
         copy.wait_send()
+
+
+def hand_over_kernel(*refs):
+    for src, dst in zip(refs[:7], refs[7:]):
+        dst[...] = src[...]
+
+
+def hand_over(*results):
+    vmem = pl.BlockSpec(memory_space=pltpu.VMEM)
+    return pl.pallas_call(
+        hand_over_kernel,
+        out_shape=tuple(jax.ShapeDtypeStruct(value.shape, value.dtype) for value in results),
+        in_specs=[vmem] * 7,
+        out_specs=(vmem,) * 7,
+    )(*results)
 
 
 def step(*operands):
@@ -526,7 +596,7 @@
             out((1, 1024), F32),
             out((64, 1024), F32),
         ),
-        in_specs=[hbm] * 4 + [vmem] * 8,
+        in_specs=[hbm] * 4 + [vmem] * 6,
         out_specs=(vmem,) * 7,
         scratch_shapes=[
             pltpu.VMEM((1024, 1024), BF16),
@@ -553,7 +623,8 @@
             pltpu.VMEM((2, 4, 4, 4, 16, 1024), BF16),
             scratch((3, 4, 4), BF16),
             scratch((4, 4), BF16),
-            scratch((3, 4), BF16),
+            scratch((2, 4), BF16),
+            scratch((2, 4), F32),
             scratch((4,), F32),
             scratch((3,), F32),
             pltpu.VMEM((4, 4, 8, 1024), F32),
@@ -595,10 +666,9 @@
     count_q, seq, width = tokens.shape
     slots = neg_row.shape[1]
     ids = (neg_owner.reshape(count_q, slots) * 1024 + neg_row).astype(F32)
-    ids = jnp.pad(ids, ((0, 0), (0, 128 - slots)), constant_values=-1.0)
-    q_half = jnp.concatenate([queries[:, :512], queries[:, 512:]], axis=0)
-    counts = jnp.broadcast_to(neg_count[:, None], (count_q, 128))
-    grad_in, g_bias_in, grad_out, g_bias_out, g_gain, g_shift, grad_table = step(
+    counts = neg_count.astype(F32)[:, None]
+    slot = jnp.concatenate([ids, counts, jnp.full((count_q, 128 - slots - 1), -1.0, F32)], axis=1)
+    results = step(
         tokens.reshape(count_q * seq, width),
         weight_in,
         weight_out,
@@ -608,10 +678,9 @@
         norm_gain[None],
         norm_shift[None],
         queries,
-        q_half,
-        ids,
-        counts,
+        slot,
     )
+    grad_in, g_bias_in, grad_out, g_bias_out, g_gain, g_shift, grad_table = hand_over(*results)
     return (grad_in, g_bias_in[0], grad_out, g_bias_out[0], g_gain[0], g_shift[0], grad_table)
 
 

time: 103 us -> 94.4 us (0.917)
  local copies, waits for them, and re-layouts: 12.4 us -> 0.16 us
  Pallas kernels: 88.1 us -> 91 us
    unnamed x7 -> x0, local copies, waits for them, and re-layouts: 9.73 us -> none
    pallas_call x0 -> x1, Pallas kernels: none -> 1.82 us  [hand_over(): pl.pallas_call(hand_over_kernel, out_shape=tuple((jax.ShapeDtypeStruct(va...]
    broadcast_in_dim x1 -> x2, local copies, waits for them, and re-layouts: 1.31 us -> 0.08 us  [the longest x1 0.08 us: body(): counts = neg_count.astype(F32)[:, None]]
    pallas_call x1, Pallas kernels: 88.1 us -> 89.2 us  [step(): pl.pallas_call(step_kernel, out_shape=(out((8, 2048), F32), out((1, 2048)...]
where the time goes in v3:
time: 94.4 us; the launch traced here: 93.9 us
  Pallas kernels  91 us (96%)
  other arithmetic  2.03 us (2%)
    pallas_call x1, Pallas kernels, step(): pl.pallas_call(step_kernel, out_shape=(out((8, 2048), F32), out((1, 2048)...  89.2 us

profile of v3, /device:TPU:0, one launch (start us, length us, event | category | flops | bytes accessed | tf_op | source)
XLA Modules:
  0.0 93.9 jit_solution(8629084910886911866)
XLA Ops:
  0.6 0.7 convert_bitcast_fusion
  1.3 0.1 pad.2.clone
  1.4 0.1 copy.20
  1.5 0.7 fusion
  2.2 0.7 maximum_maximum_fusion.slot
  2.8 89.2 %shard_map.171 = (f32[8,2048]{1,0:T(8,128)}, f32[1,2048]{1,0:T(1,128)}, f32[16,1024]{1,0:T(8,128)}, f32[1,1024]{1,0:T(1,128)}, f32[1,1024]{1,0:T(1,128)}, /*index=5*/f32[1,1024]{1,0:T(1,128)}, f32[64,1024]{1,0:T(8,128)}) custom-call(bf16[1024,1024]{1,0:T(8,128)(2,1)} %bitcast.16, bf16[1024,2048]{1,0:T(8,128)(2,1)} %win_hbm.1, bf16[2048,1024]{1,0:T(8,128)(2,1)} %wout_hbm.1, ...), custom_call_target="tpu_custom_call" | custom-call | tf_op jit(solution)/shard_map/pallas_call | solution.py:588
  92.1 1.8 %shard_map.172 = (f32[8,2048]{1,0:T(8,128)}, f32[1,2048]{1,0:T(1,128)}, f32[16,1024]{1,0:T(8,128)}, f32[1,1024]{1,0:T(1,128)}, f32[1,1024]{1,0:T(1,128)}, /*index=5*/f32[1,1024]{1,0:T(1,128)}, f32[64,1024]{1,0:T(8,128)}) custom-call(f32[8,2048]{1,0:T(8,128)} %get-tuple-element.21.refs_0_, f32[1,2048]{1,0:T(1,128)} %get-tuple-element.22.refs_1_, ...), custom_call_target="tpu_custom_call" | custom-call | tf_op jit(solution)/shard_map/pallas_call | solution.py:572
  (1 shorter events, 0.0 us)

commit v4 on v3

--- a/solution.py
+++ b/solution.py
@@ -41,7 +41,10 @@
     barrier = pltpu.get_barrier_semaphore()
     for peer in peers:
         pl.semaphore_signal(barrier, inc=1, device_id=peer, device_id_type=MESH)
-    pl.semaphore_wait(barrier, len(peers))
+
+
+def greeted(peers):
+    pl.semaphore_wait(pltpu.get_barrier_semaphore(), len(peers))
 
 
 def push(src, dst, send, recv, peer):
@@ -52,8 +55,11 @@
     return copy
 
 
-PARTS = (((0, 384), (384, 768), (768, 1024)), ((0, 384), (384, 640), (640, 1024)))
-ORDER = ((0, 1, 2), (1, 2, 0), (2, 0, 1))
+PARTS = (
+    ((0, 384), (384, 768), (768, 1024)),
+    ((0, 256), (256, 512), (512, 640), (640, 768), (768, 896), (896, 1024)),
+)
+ORDER = ((0, 1, 2), (1, 2, 0), (2, 0, 1)) * 2
 
 
 def pick(ref, axis, index, columns=None):
@@ -71,7 +77,7 @@
     g_in, g_bias_in, g_out, g_bias_out, g_gain, g_shift, g_table,
     tok, win, wout, tab, tab_own, tok_t, hidden, slope, normed, inv_std, d_sum, d_pre, bias_acc,
     qall, idall, qcol, idcol, dots, dall, turned,
-    part, r0, r1, s1, r2, t2, s2, r3, sm, cg,
+    part, r0, r1, s1, r2, s2, r3, sm, cg,
     load, sems_q, semr_q, dsem, dsemr, sem0, rsem0, sems, semr, qs, qr, cs, cr,
 ):
     here = place()
@@ -89,30 +95,33 @@
         copy.start()
         return copy
 
+    column = []
+    for j in range(4):
+        for e in range(2):
+            if j or e:
+                column.append(device(lax.rem(z + j, 4), lax.rem(k + e, 2), y, x))
+    peers = column + [moved(here, dim, j)[0] for dim in (1, 2) for j in (1, 2, 3)]
+    greet(peers)
     tok_in = local(tok_hbm, tok, 0)
     win_in = [local(win_hbm.at[:, pl.ds(512 * n, 512)], win.at[:, pl.ds(512 * n, 512)], 1 + n) for n in range(4)]
     tab_in = local(tab_hbm, tab, 5)
     wout_in = local(wout_hbm, wout, 6)
     own_in = local(tab_hbm.at[pl.ds(pl.multiple_of((y * 4 + x) * 64, 64), 64), :], tab_own, 7)
 
-    column = []
-    for j in range(4):
-        for e in range(2):
-            if j or e:
-                column.append(device(lax.rem(z + j, 4), lax.rem(k + e, 2), y, x))
-    greet(column + [moved(here, dim, j)[0] for dim in (1, 2) for j in (1, 2, 3)])
-
     query = queries[...].astype(F32)
     qall[z, k, y, x] = jnp.concatenate([query[:, :512], query[:, 512:]], axis=0).astype(BF16)
     lane = lax.broadcasted_iota(jnp.int32, (8, 128), 1)
     idall[z, k, y, x] = jnp.where(lane < 12, slot[...], -1.0)
     payload = ((0, qall), (1, idall))
-    first = []
-    for j in (1, 2, 3):
-        peer, _ = moved(here, 0, j)
-        for n, buf in payload:
-            mine = buf.at[z, k, y, x]
-            first.append(push(mine, mine, sems_q.at[0, n, j - 1], semr_q.at[0, n, j - 1], peer))
+
+    def gather_first():
+        copies = []
+        for j in (1, 2, 3):
+            peer, _ = moved(here, 0, j)
+            for n, buf in payload:
+                mine = buf.at[z, k, y, x]
+                copies.append(push(mine, mine, sems_q.at[0, n, j - 1], semr_q.at[0, n, j - 1], peer))
+        return copies
 
     def gather_second():
         for copy in first:
@@ -169,10 +178,16 @@
 
     tok_in.wait()
     win_in[0].wait()
-    lax.fori_loop(0, 2, project, 0)
+    lax.fori_loop(0, 1, project, 0)
+    greeted(peers)
+    first = gather_first()
+    lax.fori_loop(1, 2, project, 0)
+    win_in[1].wait()
+    lax.fori_loop(2, 3, project, 0)
     second = gather_second()
-    win_in[1].wait()
-    lax.fori_loop(2, 4, project, 0)
+    lax.fori_loop(3, 4, project, 0)
+    win_in[2].wait()
+    lax.fori_loop(4, 5, project, 0)
     for copy in second:
         copy.wait_recv()
     third = gather_third()
@@ -205,12 +220,9 @@
     back = [push(dots, dall.at[n], dsem.at[n], dsemr.at[n], peer) for n, peer in enumerate(column)]
     sent += back
 
-    win_in[2].wait()
+    lax.fori_loop(5, 6, project, 0)
     win_in[3].wait()
-    lax.fori_loop(4, 8, project, 0)
-
-    fourth = gather_fourth()
-    sent += fourth
+    lax.fori_loop(6, 8, project, 0)
 
     wout_in.wait()
     which = lax.broadcasted_iota(jnp.int32, (8, 1024), 0)
@@ -228,7 +240,10 @@
             carry = jnp.where(which == 2 * i + h, line, carry)
         return carry
 
-    norm_sum = lax.fori_loop(0, 4, normalise, jnp.zeros((8, 1024), F32))
+    norm_sum = lax.fori_loop(0, 2, normalise, jnp.zeros((8, 1024), F32))
+    fourth = gather_fourth()
+    sent += fourth
+    norm_sum = lax.fori_loop(2, 4, normalise, norm_sum)
 
     for copy in back:
         copy.wait_recv()
@@ -314,85 +329,70 @@
 
     def add_core(w, lo, hi, first, last):
         def one(i, carry):
-            a, e, f = i // 16, lax.rem(i // 4, 4), lax.rem(i, 4)
-            r0[w, a, e, f, :, lo:hi] = (
-                r0[w, a, e, f, :, lo:hi].astype(F32) + part[w, a, k, e, f, :, lo:hi].astype(F32)
-            ).astype(BF16)
+            a, e = i // 4, lax.rem(i, 4)
+            r0[w, a, e, :, :, lo:hi] = r0[w, a, e, :, :, lo:hi] + part[w, a, k, e, :, :, lo:hi]
             return carry
         lax.fori_loop(first, last, one, 0)
 
-    def swap(dim, w, p, step, near, far, land):
-        peer = put(here, dim, fst[dim])
-        return [
-            push(far, land[0], sems.at[step, w, p, 0], semr.at[step, w, p, 0], peer),
-            push(near, land[1], sems.at[step, w, p, 1], semr.at[step, w, p, 1], peer),
-        ]
-
-    def relay(dim, w, p, step, src, land):
-        return [push(src, land, sems.at[step, w, p, 2], semr.at[step, w, p, 2], put(here, dim, snd[dim]))]
-
     def rest(p):
         return [d for d in (0, 1, 2) if d != ORDER[p][0]]
 
     def stage_one(w, p):
         dim = ORDER[p][0]
-        cut = PARTS[w][p]
-        near, far = pick(r0.at[w], dim, fst[dim], cut), pick(r0.at[w], dim, opp[dim], cut)
-        return swap(dim, w, p, 0, near, far, (r1[w][p].at[0], r1[w][p].at[1]))
+        peer = put(here, dim, fst[dim])
+        copies = []
+        for n, to in enumerate((opp[dim], fst[dim])):
+            src = pick(r0.at[w], dim, to, PARTS[w][p])
+            copies.append(push(src, r1[w][p].at[n], sems.at[0, w, p, n], semr.at[0, w, p, n], peer))
+        return copies
 
     def relay_one(w, p):
         dim = ORDER[p][0]
         mine = pick(r0.at[w], dim, snd[dim], PARTS[w][p])
 
-        def one(i, carry):
-            e, f = i // 4, lax.rem(i, 4)
-            mine[e, f] = (mine[e, f].astype(F32) + r1[w][p][0, e, f].astype(F32)).astype(BF16)
+        def one(e, carry):
+            mine[e] = mine[e] + r1[w][p][0, e]
             return carry
-        lax.fori_loop(0, 16, one, 0)
-        return relay(dim, w, p, 0, mine, r1[w][p].at[2])
+        lax.fori_loop(0, 4, one, 0)
+        return [push(mine, r1[w][p].at[2], sems.at[0, w, p, 2], semr.at[0, w, p, 2], put(here, dim, snd[dim]))]
 
     def add_one(w, p):
         dim = ORDER[p][0]
         mine = pick(r0.at[w], dim, coord[dim], PARTS[w][p])
 
-        def one(i, carry):
-            e, f = i // 4, lax.rem(i, 4)
-            value = mine[e, f].astype(F32) + r1[w][p][1, e, f].astype(F32) + r1[w][p][2, e, f].astype(F32)
-            s1[w][p][e, f] = value.astype(BF16)
+        def one(e, carry):
+            value = mine[e].astype(F32) + r1[w][p][1, e].astype(F32) + r1[w][p][2, e].astype(F32)
+            s1[w][p][e] = value.astype(BF16)
             return carry
-        lax.fori_loop(0, 16, one, 0)
+        lax.fori_loop(0, 4, one, 0)
 
     def stage_two(w, p):
         dim = ORDER[p][1]
-        axis = rest(p).index(dim)
-        near, far = pick(s1[w][p], axis, fst[dim]), pick(s1[w][p], axis, opp[dim])
-        return swap(dim, w, p, 1, near, far, (r2[w][p].at[0], r2[w][p].at[1]))
-
-    def relay_two(w, p):
-        dim = ORDER[p][1]
-        mine = pick(s1[w][p], rest(p).index(dim), snd[dim])
-        for e in range(4):
-            t2[w][p][0, e] = mine[e].astype(F32) + r2[w][p][0, e].astype(F32)
-        return relay(dim, w, p, 1, t2[w][p].at[0], t2[w][p].at[1])
+        copies = []
+        for j in (1, 2, 3):
+            peer, to = moved(here, dim, j)
+            src = pick(s1[w][p], rest(p).index(dim), to)
+            copies.append(push(src, r2[w][p].at[j - 1], sems.at[1, w, p, j - 1], semr.at[1, w, p, j - 1], peer))
+        return copies
 
     def add_two(w, p):
         dim = ORDER[p][1]
-        mine = pick(s1[w][p], rest(p).index(dim), coord[dim])
-        for e in range(4):
-            s2[w][p][e] = mine[e].astype(F32) + r2[w][p][1, e].astype(F32) + t2[w][p][1, e]
+        value = pick(s1[w][p], rest(p).index(dim), coord[dim])[...].astype(F32)
+        for j in range(3):
+            value += r2[w][p][j].astype(F32)
+        s2[w][p][...] = value
 
     def stage_three(w, p):
         dim = ORDER[p][2]
-        return swap(dim, w, p, 2, s2[w][p].at[fst[dim]], s2[w][p].at[opp[dim]], (r3[w][p].at[0], r3[w][p].at[1]))
-
-    def relay_three(w, p):
-        dim = ORDER[p][2]
-        s2[w][p][snd[dim]] += r3[w][p][0]
-        return relay(dim, w, p, 2, s2[w][p].at[snd[dim]], r3[w][p].at[2])
+        copies = []
+        for j in (1, 2, 3):
+            peer, to = moved(here, dim, j)
+            copies.append(push(s2[w][p].at[to], r3[w][p].at[j - 1], sems.at[2, w, p, j - 1], semr.at[2, w, p, j - 1], peer))
+        return copies
 
     def add_three(w, p):
         lo, hi = PARTS[w][p]
-        value = s2[w][p][coord[ORDER[p][2]]] + r3[w][p][1] + r3[w][p][2]
+        value = s2[w][p][coord[ORDER[p][2]]] + r3[w][p][0] + r3[w][p][1] + r3[w][p][2]
         if w == 0:
             g_out[:, lo:hi] = value
         else:
@@ -425,50 +425,47 @@
     def start(step, w, p):
         groups[step][w, p] = (stage_one, stage_two, stage_three)[step](w, p)
 
-    def pass_on(step, w, p):
-        groups[step][w, p][0].wait_recv()
-        groups[step][w, p] += (relay_one, relay_two, relay_three)[step](w, p)
+    def pass_on(w, p):
+        ones[w, p][0].wait_recv()
+        ones[w, p] += relay_one(w, p)
 
     def end(step, w, p):
-        for copy in groups[step][w, p][1:]:
+        for copy in groups[step][w, p][1 if step == 0 else 0 :]:
             copy.wait_recv()
         (add_one, add_two, add_three)[step](w, p)
         if step < 2:
             start(step + 1, w, p)
 
-    def run_part(p):
-        lo, hi = PARTS[1][p]
-        lax.fori_loop(lo // 128, hi // 128, back_layer, 0)
+    def to_sibling(n, lo, hi):
         cut = pl.ds(lo, hi - lo)
-        zero[1, p] = push(
-            part.at[1, :, 1 - k, :, :, :, cut], r0.at[1, :, :, :, :, cut], sem0.at[1, p], rsem0.at[1, p], sibling
+        zero[1, n] = push(
+            part.at[1, :, 1 - k, :, :, :, cut], r0.at[1, :, :, :, :, cut], sem0.at[1, n], rsem0.at[1, n], sibling
         )
-
-    def finish_core(p):
-        zero[1, p].wait_recv()
-        add_core(1, PARTS[1][p][0], PARTS[1][p][1], 0, 64)
-        start(0, 1, p)
 
     for zz in range(4):
         zero[0, zz].wait_recv()
-        add_core(0, 0, 1024, 16 * zz, 16 * zz + 16)
+        add_core(0, 0, 1024, 4 * zz, 4 * zz + 4)
     for p in range(3):
         start(0, 0, p)
-    run_part(0)
-    for p in range(3):
-        pass_on(0, 0, p)
+    early, late = (0, 1, 2), (3, 4, 5)
+    lax.fori_loop(0, 5, back_layer, 0)
+    to_sibling(0, 0, 640)
+    for p in early:
+        pass_on(0, p)
     arrived(slope_step)
     slope_step = slopes(3)
     sent += slope_step
-    run_part(1)
-    finish_core(0)
+    lax.fori_loop(5, 6, back_layer, 0)
+    zero[1, 0].wait_recv()
+    add_core(1, 0, 640, 0, 16)
+    for p in early:
+        start(0, 1, p)
     for p in range(3):
         end(0, 0, p)
-    run_part(2)
-    finish_core(1)
-    pass_on(0, 1, 0)
-    for p in range(3):
-        pass_on(1, 0, p)
+    lax.fori_loop(6, 8, back_layer, 0)
+    to_sibling(1, 640, 1024)
+    for p in early:
+        pass_on(1, p)
 
     sm[0, k] = jnp.concatenate(
         [bias_acc[:, :1024], bias_acc[:, 1024:], grad_bias_out, grad_gain, grad_shift, jnp.zeros((3, 1024), F32)], axis=0
@@ -489,21 +486,21 @@
             copies.append(push(mine, mine, qs.at[step, j - 1], qr.at[step, j - 1], peer))
         return copies
 
-    finish_core(2)
-    pass_on(0, 1, 1)
-    end(0, 1, 0)
     for p in range(3):
         end(1, 0, p)
+    zero[1, 1].wait_recv()
+    add_core(1, 640, 1024, 0, 16)
+    for p in late:
+        start(0, 1, p)
     arrived(small)
     small = stage_small(1)
     sent += small
+    for p in early:
+        end(0, 1, p)
+    for p in late:
+        pass_on(1, p)
     arrived(slope_step)
     arrived(last)
-    pass_on(0, 1, 2)
-    end(0, 1, 1)
-    pass_on(1, 1, 0)
-    for p in range(3):
-        pass_on(2, 0, p)
 
     base = c * 1024 + (y * 4 + x) * 64
     row = (lax.broadcasted_iota(jnp.int32, (256, 128), 1) + base).astype(F32)
@@ -529,23 +526,22 @@
     unit = rows * scale
     g_table[...] = scale * (table_slope - unit * jnp.sum(unit * table_slope, axis=1, keepdims=True))
 
-    end(0, 1, 2)
-    pass_on(1, 1, 1)
+    for p in late:
+        end(0, 1, p)
     arrived(small)
     small = stage_small(2)
     sent += small
-    end(1, 1, 0)
-    pass_on(1, 1, 2)
+    for p in early:
+        end(1, 1, p)
     for p in range(3):
         end(2, 0, p)
-    end(1, 1, 1)
-    pass_on(2, 1, 0)
+    for p in late:
+        end(1, 1, p)
     arrived(small)
     small = stage_small(3)
     sent += small
-    end(1, 1, 2)
-    pass_on(2, 1, 1)
-    pass_on(2, 1, 2)
+    for p in early:
+        end(2, 1, p)
     arrived(small)
     got = ((sm[3, 0] + sm[3, 1]) + sm[3, 2]) + sm[3, 3]
     g_bias_in[:, :1024] = got[0:1]
@@ -553,7 +549,7 @@
     g_bias_out[...] = got[2:3]
     g_gain[...] = got[3:4]
     g_shift[...] = got[4:5]
-    for p in range(3):
+    for p in late:
         end(2, 1, p)
     for group in groups:
         for copies in group.values():
@@ -623,8 +619,7 @@
             pltpu.VMEM((2, 4, 4, 4, 16, 1024), BF16),
             scratch((3, 4, 4), BF16),
             scratch((4, 4), BF16),
-            scratch((2, 4), BF16),
-            scratch((2, 4), F32),
+            scratch((3, 4), BF16),
             scratch((4,), F32),
             scratch((3,), F32),
             pltpu.VMEM((4, 4, 8, 1024), F32),
@@ -636,8 +631,8 @@
             dma((7,)),
             dma((2, 4)),
             dma((2, 4)),
-            dma((3, 2, 3, 3)),
-            dma((3, 2, 3, 3)),
+            dma((3, 2, 6, 3)),
+            dma((3, 2, 6, 3)),
             dma((4, 3)),
             dma((4, 3)),
             dma((4, 3)),

time: 94.4 us -> 87.2 us (0.924)
  Pallas kernels: 91 us -> 84.1 us
    pallas_call x1, Pallas kernels: 89.2 us -> 82.3 us  [step(): pl.pallas_call(step_kernel, out_shape=(out((8, 2048), F32), out((1, 2048)...]
where the time goes in v4:
time: 87.2 us; the launch traced here: 87 us
  Pallas kernels  84.1 us (96%)
  other arithmetic  2.03 us (2%)
    pallas_call x1, Pallas kernels, step(): pl.pallas_call(step_kernel, out_shape=(out((8, 2048), F32), out((1, 2048)...  82.3 us
    pallas_call x1, Pallas kernels, hand_over(): pl.pallas_call(hand_over_kernel, out_shape=tuple((jax.ShapeDtypeStruct(va...  1.82 us

profile of v4, /device:TPU:0, one launch (start us, length us, event | category | flops | bytes accessed | tf_op | source)
XLA Modules:
  0.0 87.0 jit_solution(4612481107298158522)
XLA Ops:
  0.6 0.7 convert_bitcast_fusion
  1.3 0.1 pad.2.clone
  1.4 0.1 copy.20
  1.5 0.7 fusion
  2.2 0.7 maximum_maximum_fusion.slot
  2.8 82.3 %shard_map.171 = (f32[8,2048]{1,0:T(8,128)}, f32[1,2048]{1,0:T(1,128)}, f32[16,1024]{1,0:T(8,128)}, f32[1,1024]{1,0:T(1,128)}, f32[1,1024]{1,0:T(1,128)}, /*index=5*/f32[1,1024]{1,0:T(1,128)}, f32[64,1024]{1,0:T(8,128)}) custom-call(bf16[1024,1024]{1,0:T(8,128)(2,1)} %bitcast.16, bf16[1024,2048]{1,0:T(8,128)(2,1)} %win_hbm.1, bf16[2048,1024]{1,0:T(8,128)(2,1)} %wout_hbm.1, ...), custom_call_target="tpu_custom_call" | custom-call | tf_op jit(solution)/shard_map/pallas_call | solution.py:584
  85.1 1.8 %shard_map.172 = (f32[8,2048]{1,0:T(8,128)}, f32[1,2048]{1,0:T(1,128)}, f32[16,1024]{1,0:T(8,128)}, f32[1,1024]{1,0:T(1,128)}, f32[1,1024]{1,0:T(1,128)}, /*index=5*/f32[1,1024]{1,0:T(1,128)}, f32[64,1024]{1,0:T(8,128)}) custom-call(f32[8,2048]{1,0:T(8,128)} %get-tuple-element.21.refs_0_, f32[1,2048]{1,0:T(1,128)} %get-tuple-element.22.refs_1_, ...), custom_call_target="tpu_custom_call" | custom-call | tf_op jit(solution)/shard_map/pallas_call | solution.py:568
  (1 shorter events, 0.0 us)

commit v5 on v4

--- a/solution.py
+++ b/solution.py
@@ -183,11 +183,12 @@
     first = gather_first()
     lax.fori_loop(1, 2, project, 0)
     win_in[1].wait()
-    lax.fori_loop(2, 3, project, 0)
+    lax.fori_loop(2, 4, project, 0)
     second = gather_second()
-    lax.fori_loop(3, 4, project, 0)
     win_in[2].wait()
-    lax.fori_loop(4, 5, project, 0)
+    lax.fori_loop(4, 6, project, 0)
+    win_in[3].wait()
+    lax.fori_loop(6, 8, project, 0)
     for copy in second:
         copy.wait_recv()
     third = gather_third()
@@ -220,9 +221,6 @@
     back = [push(dots, dall.at[n], dsem.at[n], dsemr.at[n], peer) for n, peer in enumerate(column)]
     sent += back
 
-    lax.fori_loop(5, 6, project, 0)
-    win_in[3].wait()
-    lax.fori_loop(6, 8, project, 0)
 
     wout_in.wait()
     which = lax.broadcasted_iota(jnp.int32, (8, 1024), 0)
@@ -318,13 +316,17 @@
         grad_out(zz, 1 - k)
         zero[0, zz] = push(part.at[0, zz, 1 - k], r0.at[0, zz], sem0.at[0, zz], rsem0.at[0, zz], sibling)
 
+    arrived(slope_step)
+    slope_step = slopes(2)
+    sent += slope_step
+
     def own_blocks(zz, carry):
         grad_out(zz, k)
         return carry
 
     lax.fori_loop(0, 4, own_blocks, 0)
     arrived(slope_step)
-    slope_step = slopes(2)
+    slope_step = slopes(3)
     sent += slope_step
 
     def add_core(w, lo, hi, first, last):
@@ -450,23 +452,18 @@
     early, late = (0, 1, 2), (3, 4, 5)
     lax.fori_loop(0, 5, back_layer, 0)
     to_sibling(0, 0, 640)
-    for p in early:
+    for p in range(3):
         pass_on(0, p)
-    arrived(slope_step)
-    slope_step = slopes(3)
-    sent += slope_step
     lax.fori_loop(5, 6, back_layer, 0)
+    for p in range(3):
+        end(0, 0, p)
+    lax.fori_loop(6, 7, back_layer, 0)
     zero[1, 0].wait_recv()
     add_core(1, 0, 640, 0, 16)
     for p in early:
         start(0, 1, p)
-    for p in range(3):
-        end(0, 0, p)
-    lax.fori_loop(6, 8, back_layer, 0)
+    lax.fori_loop(7, 8, back_layer, 0)
     to_sibling(1, 640, 1024)
-    for p in early:
-        pass_on(1, p)
-
     sm[0, k] = jnp.concatenate(
         [bias_acc[:, :1024], bias_acc[:, 1024:], grad_bias_out, grad_gain, grad_shift, jnp.zeros((3, 1024), F32)], axis=0
     )
@@ -486,26 +483,12 @@
             copies.append(push(mine, mine, qs.at[step, j - 1], qr.at[step, j - 1], peer))
         return copies
 
-    for p in range(3):
-        end(1, 0, p)
-    zero[1, 1].wait_recv()
-    add_core(1, 640, 1024, 0, 16)
-    for p in late:
-        start(0, 1, p)
-    arrived(small)
-    small = stage_small(1)
-    sent += small
-    for p in early:
-        end(0, 1, p)
-    for p in late:
-        pass_on(1, p)
+    arrived(last)
     arrived(slope_step)
-    arrived(last)
-
     base = c * 1024 + (y * 4 + x) * 64
     row = (lax.broadcasted_iota(jnp.int32, (256, 128), 1) + base).astype(F32)
 
-    def collect(i, carry):
+    def collect(i):
         name, value = idall[i].reshape(256, 128), cg[i].reshape(256, 128)
         weight = jnp.zeros((256, 128), F32)
         for slot in range(12):
@@ -513,33 +496,50 @@
         high = weight.astype(BF16)
         low = (weight - high.astype(F32)).astype(BF16)
         some = qall[i].astype(F32).reshape(32, 16, 512)
-        halves = []
         for h in range(2):
             half = some[:, h * 8 : h * 8 + 8].reshape(256, 512).astype(BF16)
-            halves.append(dot(high, half, 0, 0) + dot(low, half, 0, 0))
-        return tuple(a + b[:64] for a, b in zip(carry, halves))
-
-    sums = lax.fori_loop(0, 4, collect, (jnp.zeros((64, 512), F32),) * 2)
-    table_slope = jnp.concatenate(sums, axis=1)
+            found = (dot(high, half, 0, 0) + dot(low, half, 0, 0))[:64]
+            at = slice(h * 512, h * 512 + 512)
+            g_table[:, at] = found if i == 0 else g_table[:, at] + found
+
+    collect(0)
+    for p in early:
+        pass_on(1, p)
+    for p in range(3):
+        end(1, 0, p)
+    arrived(small)
+    small = stage_small(1)
+    sent += small
+    zero[1, 1].wait_recv()
+    add_core(1, 640, 1024, 0, 16)
+    for p in late:
+        start(0, 1, p)
+    collect(1)
+    for p in early:
+        end(0, 1, p)
+    for p in late:
+        pass_on(1, p)
+    arrived(small)
+    small = stage_small(2)
+    sent += small
+    collect(2)
+    for p in range(3):
+        end(2, 0, p)
+    for p in late:
+        end(0, 1, p)
+    for p in early:
+        end(1, 1, p)
+    arrived(small)
+    small = stage_small(3)
+    sent += small
+    collect(3)
+    for p in late:
+        end(1, 1, p)
+    table_slope = g_table[...]
     rows = tab_own[...].astype(F32)
     scale = lax.rsqrt(jnp.sum(rows * rows, axis=1, keepdims=True) + norm_eps)
     unit = rows * scale
     g_table[...] = scale * (table_slope - unit * jnp.sum(unit * table_slope, axis=1, keepdims=True))
-
-    for p in late:
-        end(0, 1, p)
-    arrived(small)
-    small = stage_small(2)
-    sent += small
-    for p in early:
-        end(1, 1, p)
-    for p in range(3):
-        end(2, 0, p)
-    for p in late:
-        end(1, 1, p)
-    arrived(small)
-    small = stage_small(3)
-    sent += small
     for p in early:
         end(2, 1, p)
     arrived(small)

time: 87.2 us -> 87.1 us (level)
  no operation moved by 1% of the time
where the time goes in v5:
time: 87.1 us; the launch traced here: 86.9 us
  Pallas kernels  84.1 us (97%)
  other arithmetic  2.03 us (2%)
    pallas_call x1, Pallas kernels, step(): pl.pallas_call(step_kernel, out_shape=(out((8, 2048), F32), out((1, 2048)...  82.3 us
    pallas_call x1, Pallas kernels, hand_over(): pl.pallas_call(hand_over_kernel, out_shape=tuple((jax.ShapeDtypeStruct(va...  1.82 us

profile of v5, /device:TPU:0, one launch (start us, length us, event | category | flops | bytes accessed | tf_op | source)
XLA Modules:
  0.0 86.9 jit_solution(9664344825429796705)
XLA Ops:
  0.6 0.7 convert_bitcast_fusion
  1.3 0.1 pad.2.clone
  1.4 0.1 copy.20
  1.5 0.7 fusion
  2.2 0.7 maximum_maximum_fusion.slot
  2.8 82.3 %shard_map.171 = (f32[8,2048]{1,0:T(8,128)}, f32[1,2048]{1,0:T(1,128)}, f32[16,1024]{1,0:T(8,128)}, f32[1,1024]{1,0:T(1,128)}, f32[1,1024]{1,0:T(1,128)}, /*index=5*/f32[1,1024]{1,0:T(1,128)}, f32[64,1024]{1,0:T(8,128)}) custom-call(bf16[1024,1024]{1,0:T(8,128)(2,1)} %bitcast.16, bf16[1024,2048]{1,0:T(8,128)(2,1)} %win_hbm.1, bf16[2048,1024]{1,0:T(8,128)(2,1)} %wout_hbm.1, ...), custom_call_target="tpu_custom_call" | custom-call | tf_op jit(solution)/shard_map/pallas_call | solution.py:584
  85.1 1.8 %shard_map.172 = (f32[8,2048]{1,0:T(8,128)}, f32[1,2048]{1,0:T(1,128)}, f32[16,1024]{1,0:T(8,128)}, f32[1,1024]{1,0:T(1,128)}, f32[1,1024]{1,0:T(1,128)}, /*index=5*/f32[1,1024]{1,0:T(1,128)}, f32[64,1024]{1,0:T(8,128)}) custom-call(f32[8,2048]{1,0:T(8,128)} %get-tuple-element.21.refs_0_, f32[1,2048]{1,0:T(1,128)} %get-tuple-element.22.refs_1_, ...), custom_call_target="tpu_custom_call" | custom-call | tf_op jit(solution)/shard_map/pallas_call | solution.py:568
  (1 shorter events, 0.0 us)

commit v6 on v5

--- a/solution.py
+++ b/solution.py
@@ -60,6 +60,8 @@
     ((0, 256), (256, 512), (512, 640), (640, 768), (768, 896), (896, 1024)),
 )
 ORDER = ((0, 1, 2), (1, 2, 0), (2, 0, 1)) * 2
+JOINED = (((0, 0), (1, 0), (2, 0)), ((0, 384), (1, 384), (2, 256), (3, 0), (4, 0), (5, 0)))
+WIDTHS = (640, 640, 384, 128, 128, 128)
 
 
 def pick(ref, axis, index, columns=None):
@@ -76,8 +78,8 @@
     tok_hbm, win_hbm, wout_hbm, tab_hbm, bias_in, bias_out, gain, shift, queries, slot,
     g_in, g_bias_in, g_out, g_bias_out, g_gain, g_shift, g_table,
     tok, win, wout, tab, tab_own, tok_t, hidden, slope, normed, inv_std, d_sum, d_pre, bias_acc,
-    qall, idall, qcol, idcol, dots, dall, turned,
-    part, r0, r1, s1, r2, s2, r3, sm, cg,
+    qall, qcol, dots, dall, turned,
+    part, r0, r1, s1, r2, s2, r3, sm, cg, cm,
     load, sems_q, semr_q, dsem, dsemr, sem0, rsem0, sems, semr, qs, qr, cs, cr,
 ):
     here = place()
@@ -109,10 +111,16 @@
     own_in = local(tab_hbm.at[pl.ds(pl.multiple_of((y * 4 + x) * 64, 64), 64), :], tab_own, 7)
 
     query = queries[...].astype(F32)
-    qall[z, k, y, x] = jnp.concatenate([query[:, :512], query[:, 512:]], axis=0).astype(BF16)
     lane = lax.broadcasted_iota(jnp.int32, (8, 128), 1)
-    idall[z, k, y, x] = jnp.where(lane < 12, slot[...], -1.0)
-    payload = ((0, qall), (1, idall))
+    digit = jnp.floor(slot[...] * 0.0078125)
+    qall[z, k, y, x] = jnp.concatenate(
+        [
+            jnp.concatenate([query[:, :512], digit], axis=1),
+            jnp.concatenate([query[:, 512:], slot[...] - 128.0 * digit], axis=1),
+        ],
+        axis=0,
+    ).astype(BF16)
+    payload = ((0, qall),)
 
     def gather_first():
         copies = []
@@ -127,7 +135,7 @@
         for copy in first:
             copy.wait_recv()
         copies = []
-        for n, buf, dst in ((0, qall, qcol), (1, idall, idcol)):
+        for n, buf, dst in ((0, qall, qcol),):
             copies.append(push(buf.at[:, k, y, x], dst.at[k], sems_q.at[1, n, 0], semr_q.at[1, n, 0], sibling))
         for j in (1, 2, 3):
             peer, _ = moved(here, 1, j)
@@ -135,7 +143,6 @@
                 mine = buf.at[:, k, y, x]
                 copies.append(push(mine, mine, sems_q.at[2, n, j - 1], semr_q.at[2, n, j - 1], peer))
         qcol[k] = qall[:, k, y, x]
-        idcol[k] = idall[:, k, y, x]
         return copies
 
     def gather_third():
@@ -147,7 +154,7 @@
         return copies
 
     def gather_fourth():
-        for copy in third[:2]:
+        for copy in third[:1]:
             copy.wait_recv()
         copies = []
         for n, buf in payload:
@@ -196,10 +203,11 @@
 
     tab_in.wait()
     own_in.wait()
-    wide_q = qcol[...].astype(F32).reshape(8, 16, 512)
-    left = wide_q[:, :8].reshape(64, 512).astype(BF16)
-    right = wide_q[:, 8:].reshape(64, 512).astype(BF16)
-    ids = jnp.concatenate([idcol[...].reshape(64, 128), jnp.zeros((64, 128), F32)], axis=0).T[:16, :64]
+    wide_q = qcol[...].astype(F32).reshape(8, 16, 640)
+    left = wide_q[:, :8, :512].reshape(64, 512).astype(BF16)
+    right = wide_q[:, 8:, :512].reshape(64, 512).astype(BF16)
+    ids = (wide_q[:, :8, 512:] * 128.0 + wide_q[:, 8:, 512:]).reshape(64, 128)
+    ids = jnp.concatenate([ids, jnp.zeros((64, 128), F32)], axis=0).T[:16, :64]
     dots[...] = jnp.zeros_like(dots)
 
     def score_rows(i, carry):
@@ -260,7 +268,7 @@
     weights = jnp.where(live, jnp.exp(raw * q_scale / logit_divisor), 0.0)
     own = jnp.exp(positive)
     whole = own + jnp.sum(weights, axis=1, keepdims=True)
-    cg[z, k, y, x] = weights / whole / logit_divisor * q_scale
+    cg[z, k] = weights / whole / logit_divisor * q_scale
     emb_slope = ((own / whole - 1.0) / logit_divisor) * question
     d_pooled = emb_scale * (emb_slope - emb * jnp.sum(emb * emb_slope, axis=1, keepdims=True))
     grad_shift = jnp.sum(d_pooled, axis=0, keepdims=True) * 128.0
@@ -269,11 +277,15 @@
 
     def slopes(step):
         if step == 0:
-            mine = cg.at[z, k, y, x]
+            mine = cg.at[z, k]
             return [push(mine, mine, cs.at[0, 0], cr.at[0, 0], sibling)]
+        if step == 2:
+            tile = cg[0, 0]
+            for n in range(1, 8):
+                tile += pltpu.roll(cg[n // 2, n % 2], 16 * n, 1)
+            cm[y, x] = tile
         dim = step - 1
-        every = slice(None)
-        mine = cg.at[((z, every, y, x), (every, every, y, x), (every, every, every, x))[dim]]
+        mine = (cg.at[z], cm.at[y, x], cm.at[:, x])[dim]
         copies = []
         for j in (1, 2, 3):
             peer, _ = moved(here, dim, j)
@@ -298,7 +310,7 @@
         return carry + jnp.sum(ds, axis=0, keepdims=True)
 
     grad_bias_out = lax.fori_loop(0, 8, back_norm, jnp.zeros((1, 1024), F32))
-    for copy in third[2:] + fourth:
+    for copy in third[1:] + fourth:
         copy.wait_recv()
     last = gather_last()
     sent += last
@@ -361,47 +373,53 @@
     def add_one(w, p):
         dim = ORDER[p][0]
         mine = pick(r0.at[w], dim, coord[dim], PARTS[w][p])
+        g, lo = JOINED[w][p]
+        to = slice(lo, lo + PARTS[w][p][1] - PARTS[w][p][0])
 
         def one(e, carry):
             value = mine[e].astype(F32) + r1[w][p][1, e].astype(F32) + r1[w][p][2, e].astype(F32)
-            s1[w][p][e] = value.astype(BF16)
+            s1[g][e, :, :, to] = value.astype(BF16)
             return carry
         lax.fori_loop(0, 4, one, 0)
 
-    def stage_two(w, p):
-        dim = ORDER[p][1]
+    def stage_two(g):
+        dim = ORDER[g][1]
         copies = []
         for j in (1, 2, 3):
             peer, to = moved(here, dim, j)
-            src = pick(s1[w][p], rest(p).index(dim), to)
-            copies.append(push(src, r2[w][p].at[j - 1], sems.at[1, w, p, j - 1], semr.at[1, w, p, j - 1], peer))
-        return copies
-
-    def add_two(w, p):
-        dim = ORDER[p][1]
-        value = pick(s1[w][p], rest(p).index(dim), coord[dim])[...].astype(F32)
+            src = pick(s1[g], rest(g).index(dim), to)
+            copies.append(push(src, r2[g].at[j - 1], sems.at[1, 0, g, j - 1], semr.at[1, 0, g, j - 1], peer))
+        return copies
+
+    def add_two(g):
+        dim = ORDER[g][1]
+        value = pick(s1[g], rest(g).index(dim), coord[dim])[...].astype(F32)
         for j in range(3):
-            value += r2[w][p][j].astype(F32)
-        s2[w][p][...] = value
-
-    def stage_three(w, p):
-        dim = ORDER[p][2]
+            value += r2[g][j].astype(F32)
+        s2[g][...] = value
+
+    def stage_three(g):
+        dim = ORDER[g][2]
         copies = []
         for j in (1, 2, 3):
             peer, to = moved(here, dim, j)
-            copies.append(push(s2[w][p].at[to], r3[w][p].at[j - 1], sems.at[2, w, p, j - 1], semr.at[2, w, p, j - 1], peer))
-        return copies
-
-    def add_three(w, p):
-        lo, hi = PARTS[w][p]
-        value = s2[w][p][coord[ORDER[p][2]]] + r3[w][p][0] + r3[w][p][1] + r3[w][p][2]
-        if w == 0:
-            g_out[:, lo:hi] = value
-        else:
-            for n in range((hi - lo) // 128):
-                tile = value[:, n * 128 : n * 128 + 128]
-                g_in[:, 2 * lo + 256 * n : 2 * lo + 256 * n + 128] = tile[:8]
-                g_in[:, 2 * lo + 256 * n + 128 : 2 * lo + 256 * n + 256] = tile[8:]
+            copies.append(push(s2[g].at[to], r3[g].at[j - 1], sems.at[2, 0, g, j - 1], semr.at[2, 0, g, j - 1], peer))
+        return copies
+
+    def add_three(g):
+        value = s2[g][coord[ORDER[g][2]]] + r3[g][0] + r3[g][1] + r3[g][2]
+        for w in range(2):
+            for p, (lo, hi) in enumerate(PARTS[w]):
+                if JOINED[w][p][0] != g:
+                    continue
+                at = JOINED[w][p][1]
+                if w == 0:
+                    g_out[:, lo:hi] = value[:, at : at + hi - lo]
+                    continue
+                for n in range((hi - lo) // 128):
+                    tile = value[:, at + n * 128 : at + n * 128 + 128]
+                    g_in[:, 2 * lo + 256 * n : 2 * lo + 256 * n + 128] = tile[:8]
+                    g_in[:, 2 * lo + 256 * n + 128 : 2 * lo + 256 * n + 256] = tile[8:]
 
     def back_layer(n, carry):
         at = pl.ds(pl.multiple_of(n * 256, 256), 256)
@@ -422,21 +440,26 @@
         return carry
 
     ones, twos, threes = {}, {}, {}
-    groups = (ones, twos, threes)
-
-    def start(step, w, p):
-        groups[step][w, p] = (stage_one, stage_two, stage_three)[step](w, p)
+
+    def start(w, p):
+        ones[w, p] = stage_one(w, p)
 
     def pass_on(w, p):
         ones[w, p][0].wait_recv()
         ones[w, p] += relay_one(w, p)
 
-    def end(step, w, p):
-        for copy in groups[step][w, p][1 if step == 0 else 0 :]:
-            copy.wait_recv()
-        (add_one, add_two, add_three)[step](w, p)
-        if step < 2:
-            start(step + 1, w, p)
+    def end_one(w, p):
+        arrived(ones[w, p][1:])
+        add_one(w, p)
+
+    def end_two(g):
+        arrived(twos[g])
+        add_two(g)
+        threes[g] = stage_three(g)
+
+    def end_three(g):
+        arrived(threes[g])
+        add_three(g)
 
     def to_sibling(n, lo, hi):
         cut = pl.ds(lo, hi - lo)
@@ -448,7 +471,7 @@
         zero[0, zz].wait_recv()
         add_core(0, 0, 1024, 4 * zz, 4 * zz + 4)
     for p in range(3):
-        start(0, 0, p)
+        start(0, p)
     early, late = (0, 1, 2), (3, 4, 5)
     lax.fori_loop(0, 5, back_layer, 0)
     to_sibling(0, 0, 640)
@@ -456,12 +479,12 @@
         pass_on(0, p)
     lax.fori_loop(5, 6, back_layer, 0)
     for p in range(3):
-        end(0, 0, p)
+        end_one(0, p)
     lax.fori_loop(6, 7, back_layer, 0)
     zero[1, 0].wait_recv()
     add_core(1, 0, 640, 0, 16)
     for p in early:
-        start(0, 1, p)
+        start(1, p)
     lax.fori_loop(7, 8, back_layer, 0)
     to_sibling(1, 640, 1024)
     sm[0, k] = jnp.concatenate(
@@ -489,15 +512,17 @@
     row = (lax.broadcasted_iota(jnp.int32, (256, 128), 1) + base).astype(F32)
 
     def collect(i):
-        name, value = idall[i].reshape(256, 128), cg[i].reshape(256, 128)
+        some = qall[i].astype(F32).reshape(32, 16, 640)
+        name = (some[:, :8, 512:] * 128.0 + some[:, 8:, 512:]).reshape(256, 128)
+        tiles = cm[...].reshape(128, 128)
+        value = jnp.concatenate([pltpu.roll(tiles, (128 - 16 * n) % 128, 1) for n in (2 * i, 2 * i + 1)], axis=0)
         weight = jnp.zeros((256, 128), F32)
         for slot in range(12):
             weight += jnp.where(name[:, slot : slot + 1] == row, value[:, slot : slot + 1], 0.0)
         high = weight.astype(BF16)
         low = (weight - high.astype(F32)).astype(BF16)
-        some = qall[i].astype(F32).reshape(32, 16, 512)
         for h in range(2):
-            half = some[:, h * 8 : h * 8 + 8].reshape(256, 512).astype(BF16)
+            half = some[:, h * 8 : h * 8 + 8, :512].reshape(256, 512).astype(BF16)
             found = (dot(high, half, 0, 0) + dot(low, half, 0, 0))[:64]
             at = slice(h * 512, h * 512 + 512)
             g_table[:, at] = found if i == 0 else g_table[:, at] + found
@@ -505,43 +530,41 @@
     collect(0)
     for p in early:
         pass_on(1, p)
-    for p in range(3):
-        end(1, 0, p)
     arrived(small)
     small = stage_small(1)
     sent += small
     zero[1, 1].wait_recv()
     add_core(1, 640, 1024, 0, 16)
     for p in late:
-        start(0, 1, p)
+        start(1, p)
     collect(1)
     for p in early:
-        end(0, 1, p)
+        end_one(1, p)
+        twos[p] = stage_two(p)
     for p in late:
         pass_on(1, p)
     arrived(small)
     small = stage_small(2)
     sent += small
     collect(2)
-    for p in range(3):
-        end(2, 0, p)
     for p in late:
-        end(0, 1, p)
+        end_one(1, p)
+        twos[p] = stage_two(p)
     for p in early:
-        end(1, 1, p)
+        end_two(p)
     arrived(small)
     small = stage_small(3)
     sent += small
     collect(3)
     for p in late:
-        end(1, 1, p)
+        end_two(p)
     table_slope = g_table[...]
     rows = tab_own[...].astype(F32)
     scale = lax.rsqrt(jnp.sum(rows * rows, axis=1, keepdims=True) + norm_eps)
     unit = rows * scale
     g_table[...] = scale * (table_slope - unit * jnp.sum(unit * table_slope, axis=1, keepdims=True))
     for p in early:
-        end(2, 1, p)
+        end_three(p)
     arrived(small)
     got = ((sm[3, 0] + sm[3, 1]) + sm[3, 2]) + sm[3, 3]
     g_bias_in[:, :1024] = got[0:1]
@@ -550,8 +573,8 @@
     g_gain[...] = got[3:4]
     g_shift[...] = got[4:5]
     for p in late:
-        end(2, 1, p)
-    for group in groups:
+        end_three(p)
+    for group in (ones, twos, threes):
         for copies in group.values():
             sent += copies
     for copy in sent + list(zero.values()):
@@ -578,6 +601,9 @@
 
     def scratch(shape, kind):
         return tuple(tuple(pltpu.VMEM(shape + (16, hi - lo), kind) for lo, hi in row) for row in PARTS)
+
+    def joined(shape, kind):
+        return tuple(pltpu.VMEM(shape + (16, width), kind) for width in WIDTHS)
 
     dma = pltpu.SemaphoreType.DMA
     out = jax.ShapeDtypeStruct
@@ -608,25 +634,24 @@
             pltpu.VMEM((1024, 1024), BF16),
             pltpu.VMEM((1024, 256), BF16),
             pltpu.VMEM((1, 2048), F32),
-            pltpu.VMEM((4, 2, 4, 4, 16, 512), BF16),
-            pltpu.VMEM((4, 2, 4, 4, 8, 128), F32),
-            pltpu.VMEM((2, 4, 16, 512), BF16),
-            pltpu.VMEM((2, 4, 8, 128), F32),
+            pltpu.VMEM((4, 2, 4, 4, 16, 640), BF16),
+            pltpu.VMEM((2, 4, 16, 640), BF16),
             pltpu.VMEM((16, 128), F32),
             pltpu.VMEM((7, 16, 128), F32),
             pltpu.VMEM((128, 128), F32),
             pltpu.VMEM((2, 4, 2, 4, 4, 16, 1024), BF16),
             pltpu.VMEM((2, 4, 4, 4, 16, 1024), BF16),
             scratch((3, 4, 4), BF16),
-            scratch((4, 4), BF16),
-            scratch((3, 4), BF16),
-            scratch((4,), F32),
-            scratch((3,), F32),
+            joined((4, 4), BF16),
+            joined((3, 4), BF16),
+            joined((4,), F32),
+            joined((3,), F32),
             pltpu.VMEM((4, 4, 8, 1024), F32),
-            pltpu.VMEM((4, 2, 4, 4, 8, 128), F32),
+            pltpu.VMEM((4, 2, 8, 128), F32),
+            pltpu.VMEM((4, 4, 8, 128), F32),
             dma((8,)),
-            dma((5, 2, 3)),
-            dma((5, 2, 3)),
+            dma((5, 1, 3)),
+            dma((5, 1, 3)),
             dma((7,)),
             dma((7,)),
             dma((2, 4)),

time: 87.1 us -> 87.8 us (level)
  no operation moved by 1% of the time
where the time goes in v6:
time: 87.8 us; the launch traced here: 87.6 us
  Pallas kernels  84.7 us (96%)
  other arithmetic  2.03 us (2%)
    pallas_call x1, Pallas kernels, step(): pl.pallas_call(step_kernel, out_shape=(out((8, 2048), F32), out((1, 2048)...  82.9 us
    pallas_call x1, Pallas kernels, hand_over(): pl.pallas_call(hand_over_kernel, out_shape=tuple((jax.ShapeDtypeStruct(va...  1.82 us

profile of v6, /device:TPU:0, one launch (start us, length us, event | category | flops | bytes accessed | tf_op | source)
XLA Modules:
  0.0 87.6 jit_solution(18010089102599793678)
XLA Ops:
  0.6 0.7 convert_bitcast_fusion
  1.3 0.1 pad.2.clone
  1.4 0.1 copy.20
  1.5 0.7 fusion
  2.2 0.7 maximum_maximum_fusion.slot
  2.8 82.9 %shard_map.171 = (f32[8,2048]{1,0:T(8,128)}, f32[1,2048]{1,0:T(1,128)}, f32[16,1024]{1,0:T(8,128)}, f32[1,1024]{1,0:T(1,128)}, f32[1,1024]{1,0:T(1,128)}, /*index=5*/f32[1,1024]{1,0:T(1,128)}, f32[64,1024]{1,0:T(8,128)}) custom-call(bf16[1024,1024]{1,0:T(8,128)(2,1)} %bitcast.16, bf16[1024,2048]{1,0:T(8,128)(2,1)} %win_hbm.1, bf16[2048,1024]{1,0:T(8,128)(2,1)} %wout_hbm.1, ...), custom_call_target="tpu_custom_call" | custom-call | tf_op jit(solution)/shard_map/pallas_call | solution.py:610
  85.7 1.8 %shard_map.172 = (f32[8,2048]{1,0:T(8,128)}, f32[1,2048]{1,0:T(1,128)}, f32[16,1024]{1,0:T(8,128)}, f32[1,1024]{1,0:T(1,128)}, f32[1,1024]{1,0:T(1,128)}, /*index=5*/f32[1,1024]{1,0:T(1,128)}, f32[64,1024]{1,0:T(8,128)}) custom-call(f32[8,2048]{1,0:T(8,128)} %get-tuple-element.21.refs_0_, f32[1,2048]{1,0:T(1,128)} %get-tuple-element.22.refs_1_, ...), custom_call_target="tpu_custom_call" | custom-call | tf_op jit(solution)/shard_map/pallas_call | solution.py:591
  (1 shorter events, 0.0 us)

commit v7 on v6

--- a/solution.py
+++ b/solution.py
@@ -351,8 +351,12 @@
     def rest(p):
         return [d for d in (0, 1, 2) if d != ORDER[p][0]]
 
+    def sides(w, p):
+        return (snd, fst) if w == 1 and p > 2 else (fst, snd)
+
     def stage_one(w, p):
         dim = ORDER[p][0]
+        fst, snd = sides(w, p)
         peer = put(here, dim, fst[dim])
         copies = []
         for n, to in enumerate((opp[dim], fst[dim])):
@@ -362,6 +366,7 @@
 
     def relay_one(w, p):
         dim = ORDER[p][0]
+        fst, snd = sides(w, p)
         mine = pick(r0.at[w], dim, snd[dim], PARTS[w][p])
 
         def one(e, carry):

time: 87.8 us -> 87.7 us (level)
  no operation moved by 1% of the time
where the time goes in v7:
time: 87.7 us; the launch traced here: 87.4 us
  Pallas kernels  84.6 us (96%)
  other arithmetic  2.03 us (2%)
    pallas_call x1, Pallas kernels, step(): pl.pallas_call(step_kernel, out_shape=(out((8, 2048), F32), out((1, 2048)...  82.8 us
    pallas_call x1, Pallas kernels, hand_over(): pl.pallas_call(hand_over_kernel, out_shape=tuple((jax.ShapeDtypeStruct(va...  1.82 us

profile of v7, /device:TPU:0, one launch (start us, length us, event | category | flops | bytes accessed | tf_op | source)
XLA Modules:
  0.0 87.4 jit_solution(3122428353550789290)
XLA Ops:
  0.6 0.7 convert_bitcast_fusion
  1.3 0.1 pad.2.clone
  1.4 0.1 copy.20
  1.5 0.7 fusion
  2.2 0.7 maximum_maximum_fusion.slot
  2.8 82.8 %shard_map.171 = (f32[8,2048]{1,0:T(8,128)}, f32[1,2048]{1,0:T(1,128)}, f32[16,1024]{1,0:T(8,128)}, f32[1,1024]{1,0:T(1,128)}, f32[1,1024]{1,0:T(1,128)}, /*index=5*/f32[1,1024]{1,0:T(1,128)}, f32[64,1024]{1,0:T(8,128)}) custom-call(bf16[1024,1024]{1,0:T(8,128)(2,1)} %bitcast.16, bf16[1024,2048]{1,0:T(8,128)(2,1)} %win_hbm.1, bf16[2048,1024]{1,0:T(8,128)(2,1)} %wout_hbm.1, ...), custom_call_target="tpu_custom_call" | custom-call | tf_op jit(solution)/shard_map/pallas_call | solution.py:615
  85.6 1.8 %shard_map.172 = (f32[8,2048]{1,0:T(8,128)}, f32[1,2048]{1,0:T(1,128)}, f32[16,1024]{1,0:T(8,128)}, f32[1,1024]{1,0:T(1,128)}, f32[1,1024]{1,0:T(1,128)}, /*index=5*/f32[1,1024]{1,0:T(1,128)}, f32[64,1024]{1,0:T(8,128)}) custom-call(f32[8,2048]{1,0:T(8,128)} %get-tuple-element.21.refs_0_, f32[1,2048]{1,0:T(1,128)} %get-tuple-element.22.refs_1_, ...), custom_call_target="tpu_custom_call" | custom-call | tf_op jit(solution)/shard_map/pallas_call | solution.py:596
  (1 shorter events, 0.0 us)

commit v8 on v6

--- a/solution.py
+++ b/solution.py
@@ -312,8 +312,6 @@
     grad_bias_out = lax.fori_loop(0, 8, back_norm, jnp.zeros((1, 1024), F32))
     for copy in third[1:] + fourth:
         copy.wait_recv()
-    last = gather_last()
-    sent += last
     arrived(slope_step)
     slope_step = slopes(1)
     sent += slope_step
@@ -473,8 +471,12 @@
     for p in range(3):
         start(0, p)
     early, late = (0, 1, 2), (3, 4, 5)
-    lax.fori_loop(0, 5, back_layer, 0)
-    to_sibling(0, 0, 640)
+    last = gather_last()
+    sent += last
+    lax.fori_loop(0, 3, back_layer, 0)
+    to_sibling(0, 0, 384)
+    lax.fori_loop(3, 5, back_layer, 0)
+    to_sibling(2, 384, 640)
     for p in range(3):
         pass_on(0, p)
     lax.fori_loop(5, 6, back_layer, 0)
@@ -482,6 +484,7 @@
         end_one(0, p)
     lax.fori_loop(6, 7, back_layer, 0)
     zero[1, 0].wait_recv()
+    zero[1, 2].wait_recv()
     add_core(1, 0, 640, 0, 16)
     for p in early:
         start(1, p)

time: 87.8 us -> 87.9 us (level)
  no operation moved by 1% of the time
where the time goes in v8:
time: 87.9 us; the launch traced here: 87.6 us
  Pallas kernels  84.8 us (96%)
  other arithmetic  2.03 us (2%)
    pallas_call x1, Pallas kernels, step(): pl.pallas_call(step_kernel, out_shape=(out((8, 2048), F32), out((1, 2048)...  83 us
    pallas_call x1, Pallas kernels, hand_over(): pl.pallas_call(hand_over_kernel, out_shape=tuple((jax.ShapeDtypeStruct(va...  1.82 us

profile of v8, /device:TPU:0, one launch (start us, length us, event | category | flops | bytes accessed | tf_op | source)
XLA Modules:
  0.0 87.6 jit_solution(1643537106217349347)
XLA Ops:
  0.6 0.7 convert_bitcast_fusion
  1.3 0.1 pad.2.clone
  1.4 0.1 copy.20
  1.5 0.7 fusion
  2.2 0.7 maximum_maximum_fusion.slot
  2.8 83.0 %shard_map.171 = (f32[8,2048]{1,0:T(8,128)}, f32[1,2048]{1,0:T(1,128)}, f32[16,1024]{1,0:T(8,128)}, f32[1,1024]{1,0:T(1,128)}, f32[1,1024]{1,0:T(1,128)}, /*index=5*/f32[1,1024]{1,0:T(1,128)}, f32[64,1024]{1,0:T(8,128)}) custom-call(bf16[1024,1024]{1,0:T(8,128)(2,1)} %bitcast.16, bf16[1024,2048]{1,0:T(8,128)(2,1)} %win_hbm.1, bf16[2048,1024]{1,0:T(8,128)(2,1)} %wout_hbm.1, ...), custom_call_target="tpu_custom_call" | custom-call | tf_op jit(solution)/shard_map/pallas_call | solution.py:613
  85.8 1.8 %shard_map.172 = (f32[8,2048]{1,0:T(8,128)}, f32[1,2048]{1,0:T(1,128)}, f32[16,1024]{1,0:T(8,128)}, f32[1,1024]{1,0:T(1,128)}, f32[1,1024]{1,0:T(1,128)}, /*index=5*/f32[1,1024]{1,0:T(1,128)}, f32[64,1024]{1,0:T(8,128)}) custom-call(f32[8,2048]{1,0:T(8,128)} %get-tuple-element.21.refs_0_, f32[1,2048]{1,0:T(1,128)} %get-tuple-element.22.refs_1_, ...), custom_call_target="tpu_custom_call" | custom-call | tf_op jit(solution)/shard_map/pallas_call | solution.py:594
  (1 shorter events, 0.0 us)

commit v9 on v6

--- a/solution.py
+++ b/solution.py
@@ -401,13 +401,27 @@
     def stage_three(g):
         dim = ORDER[g][2]
         copies = []
+        if g < 3:
+            for n, to in enumerate((opp[dim], fst[dim])):
+                land, peer = r3[g].at[n], put(here, dim, fst[dim])
+                copies.append(push(s2[g].at[to], land, sems.at[2, 0, g, n], semr.at[2, 0, g, n], peer))
+            return copies
         for j in (1, 2, 3):
             peer, to = moved(here, dim, j)
             copies.append(push(s2[g].at[to], r3[g].at[j - 1], sems.at[2, 0, g, j - 1], semr.at[2, 0, g, j - 1], peer))
         return copies
 
+    def relay_three(g):
+        dim = ORDER[g][2]
+        threes[g][0].wait_recv()
+        s2[g][snd[dim]] += r3[g][0]
+        src, peer = s2[g].at[snd[dim]], put(here, dim, snd[dim])
+        threes[g].append(push(src, r3[g].at[2], sems.at[2, 0, g, 2], semr.at[2, 0, g, 2], peer))
+
     def add_three(g):
-        value = s2[g][coord[ORDER[g][2]]] + r3[g][0] + r3[g][1] + r3[g][2]
+        value = s2[g][coord[ORDER[g][2]]] + r3[g][1] + r3[g][2]
+        if g > 2:
+            value += r3[g][0]
         for w in range(2):
             for p, (lo, hi) in enumerate(PARTS[w]):
                 if JOINED[w][p][0] != g:
@@ -458,7 +472,7 @@
         threes[g] = stage_three(g)
 
     def end_three(g):
-        arrived(threes[g])
+        arrived(threes[g][1:] if g < 3 else threes[g])
         add_three(g)
 
     def to_sibling(n, lo, hi):
@@ -556,6 +570,8 @@
     small = stage_small(3)
     sent += small
     collect(3)
+    for g in early:
+        relay_three(g)
     for p in late:
         end_two(p)
     table_slope = g_table[...]

time: 87.8 us -> 87.8 us (level)
  no operation moved by 1% of the time
where the time goes in v9:
time: 87.8 us; the launch traced here: 87.5 us
  Pallas kernels  84.7 us (96%)
  other arithmetic  2.03 us (2%)
    pallas_call x1, Pallas kernels, step(): pl.pallas_call(step_kernel, out_shape=(out((8, 2048), F32), out((1, 2048)...  82.9 us
    pallas_call x1, Pallas kernels, hand_over(): pl.pallas_call(hand_over_kernel, out_shape=tuple((jax.ShapeDtypeStruct(va...  1.82 us

profile of v9, /device:TPU:0, one launch (start us, length us, event | category | flops | bytes accessed | tf_op | source)
XLA Modules:
  0.0 87.5 jit_solution(16130152448204888769)
XLA Ops:
  0.6 0.7 convert_bitcast_fusion
  1.3 0.1 pad.2.clone
  1.4 0.1 copy.20
  1.5 0.7 fusion
  2.2 0.7 maximum_maximum_fusion.slot
  2.8 82.9 %shard_map.171 = (f32[8,2048]{1,0:T(8,128)}, f32[1,2048]{1,0:T(1,128)}, f32[16,1024]{1,0:T(8,128)}, f32[1,1024]{1,0:T(1,128)}, f32[1,1024]{1,0:T(1,128)}, /*index=5*/f32[1,1024]{1,0:T(1,128)}, f32[64,1024]{1,0:T(8,128)}) custom-call(bf16[1024,1024]{1,0:T(8,128)(2,1)} %bitcast.16, bf16[1024,2048]{1,0:T(8,128)(2,1)} %win_hbm.1, bf16[2048,1024]{1,0:T(8,128)(2,1)} %wout_hbm.1, ...), custom_call_target="tpu_custom_call" | custom-call | tf_op jit(solution)/shard_map/pallas_call | solution.py:626
  85.7 1.8 %shard_map.172 = (f32[8,2048]{1,0:T(8,128)}, f32[1,2048]{1,0:T(1,128)}, f32[16,1024]{1,0:T(8,128)}, f32[1,1024]{1,0:T(1,128)}, f32[1,1024]{1,0:T(1,128)}, /*index=5*/f32[1,1024]{1,0:T(1,128)}, f32[64,1024]{1,0:T(8,128)}) custom-call(f32[8,2048]{1,0:T(8,128)} %get-tuple-element.21.refs_0_, f32[1,2048]{1,0:T(1,128)} %get-tuple-element.22.refs_1_, ...), custom_call_target="tpu_custom_call" | custom-call | tf_op jit(solution)/shard_map/pallas_call | solution.py:607
  (1 shorter events, 0.0 us)
